TPU v7x, 256 devices: a whole 4x4x8 slice. The times are simulated.
256 devices in a mesh: row: 64 (over z, x, core), col: 4 (over y).
Axes of the slice: x: 4, y: 4, z: 8, core: 2. Of those that a mesh axis runs over, the one named last changes fastest.
Arguments:
- diagonal: float32 [256, 512, 512], P(('row', 'col')), may hold values from -0.05 to 1.05
- lower: float32 [256, 512, 512], P(('row', 'col')), may hold values from -1 to 1, as said below
- upper: float32 [256, 512, 512], P(('row', 'col')), may hold values from -1 to 1, as said below
- right_side: float32 [256, 512, 128], P(('row', 'col')), may hold values from -6 to 6
- guess: float32 [256, 512, 128], P(('row', 'col')), may hold values from -4 to 4
Outputs:
- solution: float32 [256, 512, 128], P(('row', 'col'))
Inputs may be any that keep to these rules, and one draw needn't show every extreme that they name: `lower`: each block is one half of an orthogonal matrix. `upper`: each block is one half of an orthogonal matrix.
All inputs are finite; a program needn't handle non-finite values.
Results may differ from a plain program's by a relative error of at most 0.00026.
Values sent between devices are 32-bit elements; how exact they have to be, the bound alone decides.
No kernel may reach another device: no remote copies, remote signals or barrier semaphores. Data moves between devices by JAX's collectives and lax.ppermute only.
A program may use at most 64 MiB of HBM per device.

v0:
```python
import jax
import jax.numpy as jnp
from jax import lax
from jax.sharding import PartitionSpec as P

AXES = ("row", "col")


def shifted(value, steps):
    count = lax.axis_size(AXES)
    initial, last = (max(0, -steps), min(count, count - steps))
    return lax.ppermute(value, AXES, [(source, source + steps) for source in range(initial, last)])


def multiply(left, right):
    return jnp.dot(left, right, precision=lax.Precision.HIGH, preferred_element_type=jnp.float32)


def residual(matrix):
    order = matrix.shape[-1]
    scale = order / jnp.trace(matrix)
    return jnp.eye(order, dtype=jnp.float32) - matrix * scale, scale


def invert(matrix):
    rest, scale = residual(matrix)
    square = multiply(rest, rest)
    eye = jnp.eye(matrix.shape[-1], dtype=jnp.float32)
    return (eye + rest + square + multiply(rest, square)) * scale


def body(diagonal, lower, upper, right_side, guess):
    chain = lax.axis_size(AXES)
    place = lax.axis_index(AXES)
    diag = diagonal[0]
    low = jnp.where(place == 0, jnp.float32(0.0), lower[0])
    up = jnp.where(place == chain - 1, jnp.float32(0.0), upper[0])
    rhs = right_side[0]
    cols = rhs.shape[1]
    guess_l = shifted(guess[0], 1)
    guess_r = shifted(guess[0], -1)
    pivot = invert(diag)
    scaled_up = multiply(pivot, up)
    scaled_low = multiply(pivot, low)
    up_l = shifted(scaled_up, 1)
    low_r = shifted(scaled_low, -1)
    scaled_rhs = multiply(pivot, rhs)
    vec_l = shifted(jnp.concatenate([scaled_rhs, multiply(scaled_low, guess_l)], axis=1), 1)
    vec_r = shifted(jnp.concatenate([scaled_rhs, multiply(scaled_up, guess_r)], axis=1), -1)
    diag1 = diag - multiply(low, up_l) - multiply(up, low_r)
    pivot1 = invert(diag1)
    next_l = shifted(multiply(pivot1, up), 1)
    next_r = shifted(multiply(pivot1, low), -1)
    lv = multiply(low, vec_l)
    uv = multiply(up, vec_r)
    rhs1 = rhs - lv[:, :cols] - uv[:, :cols]
    w_l = shifted(multiply(pivot1, rhs1 + lv[:, cols:]), 1)
    w_r = shifted(multiply(pivot1, rhs1 + uv[:, cols:]), -1)
    pass_l = shifted(multiply(scaled_low, next_l), 1)
    pass_r = shifted(multiply(scaled_up, next_r), -1)
    d_l = shifted(multiply(scaled_low, w_l), 1)
    d_r = shifted(multiply(scaled_up, w_r), -1)
    diag2 = diag1 - multiply(multiply(low, pass_l), up_l) - multiply(multiply(up, pass_r), low_r)
    inner = rhs1 + multiply(low, d_l) + multiply(up, d_r)
    rest, scale = residual(diag2)
    part = inner + multiply(rest, multiply(rest, inner))
    return ((part + multiply(rest, part)) * scale)[None]


def solution(mesh):
    spec = P(AXES, None, None)
    return jax.shard_map(
        body,
        mesh=mesh,
        in_specs=(spec,) * 5,
        out_specs=spec,
        check_vma=False,
    )
```

profile of v0, /device:TPU:129, one launch (start us, length us, event | category | flops | bytes accessed | tf_op | source)
XLA Modules:
  0.0 155.9 jit_solution(15679771422662110593)
XLA Ops:
  0.0 5.3 %collective-permute-start.2 = (f32[512,128]{1,0:T(8,128)}, f32[512,128]{1,0:T(8,128)S(1)}, u32[]{:S(2)}, u32[]{:S(2)}) collective-permute-start(f32[512,128]{1,0:T(8,128)} %bitcast.86), channel_id=1, source_target_pairs={{1,0},{2,1},{3,2},{4,3},{5,4},{6,5},{7,6},{8,7},{9,8},{10,9},{11,1... | collective-permute-start | bytes 786440 | tf_op jit(solution)/shard_map/ppermute | solution.py:12
  5.3 1.9 %collective-permute-start = (f32[512,128]{1,0:T(8,128)}, f32[512,128]{1,0:T(8,128)}, u32[]{:S(2)}, u32[]{:S(2)}) collective-permute-start(f32[512,128]{1,0:T(8,128)} %bitcast.87), channel_id=1, source_target_pairs={{0,1},{1,2},{2,3},{3,4},{4,5},{5,6},{6,7},{7,8},{8,9},{9,10},{10,1... | collective-permute-start | bytes 786440 | tf_op jit(solution)/shard_map/ppermute | solution.py:12
  7.3 1.9 %fusion.21 = f32[]{:T(128)} fusion(f32[1,512,512]{2,1,0:T(8,128)} %param.5), kind=kLoop, calls=%fused_computation.35 | loop fusion | flops 786431 | bytes 1048580 | tf_op jit(solution)/shard_map/jit(trace)/reduce_sum | solution.py:21
  9.9 1.1 fusion.19
  10.9 0.0 copy-start.1
  10.9 1.1 fusion.3
  12.1 0.1 copy-done.1
  12.2 1.0 fusion.17
  13.2 0.2 copy-done
  13.4 1.0 fusion.30
  14.4 0.1 copy-done.15
  14.5 0.7 fusion.82
  15.2 0.0 collective-permute-done
  15.2 1.6 %fusion.96 = f32[512,128]{0,1:T(8,128)S(1)} fusion(f32[512,512]{1,0:T(8,128)S(1)} %fusion.30, f32[512,128]{1,0:T(8,128)} %collective-permute-done), kind=kOutput, calls=%fused_computation.121 | convolution fusion | flops 201326592 | bytes 1572864 | tf_op jit(solution)/shard_map/dot_general | solution.py:16
  16.8 0.0 collective-permute-done.2
  16.8 0.7 fusion.97
  17.5 0.1 pad_maximum_fusion.1
  17.6 1.9 %collective-permute-start.1 = (f32[512,256]{0,1:T(8,128)S(1)}, f32[512,256]{0,1:T(8,128)S(1)}, u32[]{:S(2)}, u32[]{:S(2)}) collective-permute-start(f32[512,256]{0,1:T(8,128)S(1)} %get-tuple-element.5), channel_id=1, source_target_pairs={{0,1},{1,2},{2,3},{3,4},{4,5},{5,6},{6,7},{7,8},{8,9},{9,10},{10,1... | collective-permute-start | bytes 1572872 | tf_op jit(solution)/shard_map/ppermute | solution.py:12
  19.5 4.9 %collective-permute-start.3 = (f32[512,256]{0,1:T(8,128)S(1)}, f32[512,256]{0,1:T(8,128)S(1)}, u32[]{:S(2)}, u32[]{:S(2)}) collective-permute-start(f32[512,256]{0,1:T(8,128)S(1)} %get-tuple-element.6), channel_id=1, source_target_pairs={{1,0},{2,1},{3,2},{4,3},{5,4},{6,5},{7,6},{8,7},{9,8},{10,9},{11,1... | collective-permute-start | bytes 1572872 | tf_op jit(solution)/shard_map/ppermute | solution.py:12
  24.4 3.9 %collective-permute-start.5 = (f32[512,512]{1,0:T(8,128)S(1)}, f32[512,512]{1,0:T(8,128)S(1)}, u32[]{:S(2)}, u32[]{:S(2)}) collective-permute-start(f32[512,512]{1,0:T(8,128)S(1)} %fusion.30), channel_id=1, source_target_pairs={{1,0},{2,1},{3,2},{4,3},{5,4},{6,5},{7,6},{8,7},{9,8},{10,9},{11,1... | collective-permute-start | bytes 3145736 | tf_op jit(solution)/shard_map/ppermute | solution.py:12
  28.3 2.1 %collective-permute-start.4 = (f32[512,512]{1,0:T(8,128)S(1)}, f32[512,512]{1,0:T(8,128)S(1)}, u32[]{:S(2)}, u32[]{:S(2)}) collective-permute-start(f32[512,512]{1,0:T(8,128)S(1)} %fusion.17), channel_id=1, source_target_pairs={{0,1},{1,2},{2,3},{3,4},{4,5},{5,6},{6,7},{7,8},{8,9},{9,10},{10,1... | collective-permute-start | bytes 3145736 | tf_op jit(solution)/shard_map/ppermute | solution.py:12
  30.4 0.0 collective-permute-done.1
  30.4 0.6 fusion.28
  31.1 16.3 %collective-permute-done.3 = f32[512,256]{0,1:T(8,128)S(1)} collective-permute-done((f32[512,256]{0,1:T(8,128)S(1)}, f32[512,256]{0,1:T(8,128)S(1)}, u32[]{:S(2)}, u32[]{:S(2)}) %collective-permute-start.3) | collective-permute-done | bytes 524320 | tf_op jit(solution)/shard_map/ppermute | solution.py:12
  47.3 0.6 fusion.15
  48.0 0.1 slice_subtract_fusion
  48.0 0.7 copy-done.13
  48.8 9.8 %collective-permute-done.5 = f32[512,512]{1,0:T(8,128)S(1)} collective-permute-done((f32[512,512]{1,0:T(8,128)S(1)}, f32[512,512]{1,0:T(8,128)S(1)}, u32[]{:S(2)}, u32[]{:S(2)}) %collective-permute-start.5) | collective-permute-done | bytes 1048608 | tf_op jit(solution)/shard_map/ppermute | solution.py:12
  58.6 1.0 fusion.13
  59.6 0.8 collective-permute-done.4
  60.5 2.7 %select_reduce_fusion.1 = (f32[]{:T(128)}, f32[512,512]{1,0:T(8,128)}) fusion(f32[512,512]{1,0:T(8,128)S(1)} %fusion.13, f32[512,512]{1,0:T(8,128)S(1)} %collective-permute-done.4, f32[1,512,512]{2,1,0:T(8,128)S(1)} %copy-done, pred[]{:T(512)S(6)} %eq.41, f32[1,512,512]{2,1,0:T(8,128)S(1)} %copy-done.5), kind=kOutput, calls=%fused_computation.47 | convolution fusion | flops 806879232 | bytes 5242885 | tf_op jit(solution)/shard_map/dot_general | solution.py:16
  63.8 2.7 %fusion.35 = f32[512,512]{1,0:T(8,128)S(1)} fusion(f32[512,512]{1,0:T(8,128)} %get-tuple-element.8, f32[]{:T(128)S(6)} %div.10), kind=kOutput, calls=%fused_computation.53 | convolution fusion | flops 806354944 | bytes 2097156 | tf_op jit(solution)/shard_map/dot_general | solution.py:16
  66.5 1.1 fusion.1
  67.7 1.0 fusion.9
  68.7 2.9 %collective-permute-start.10 = (f32[512,512]{1,0:T(8,128)S(1)}, f32[512,512]{1,0:T(8,128)S(1)}, u32[]{:S(2)}, u32[]{:S(2)}) collective-permute-start(f32[512,512]{1,0:T(8,128)S(1)} %fusion.9), channel_id=1, source_target_pairs={{0,1},{1,2},{2,3},{3,4},{4,5},{5,6},{6,7},{7,8},{8,9},{9,10},{10,1... | collective-permute-start | bytes 3145736 | tf_op jit(solution)/shard_map/ppermute | solution.py:12
  71.7 1.0 fusion.22
  72.7 4.1 %collective-permute-start.12 = (f32[512,512]{1,0:T(8,128)S(1)}, f32[512,512]{1,0:T(8,128)S(1)}, u32[]{:S(2)}, u32[]{:S(2)}) collective-permute-start(f32[512,512]{1,0:T(8,128)S(1)} %fusion.22), channel_id=1, source_target_pairs={{1,0},{2,1},{3,2},{4,3},{5,4},{6,5},{7,6},{8,7},{9,8},{10,9},{11,1... | collective-permute-start | bytes 3145736 | tf_op jit(solution)/shard_map/ppermute | solution.py:12
  76.8 0.6 fusion.80
  77.4 4.0 %collective-permute-start.8 = (f32[512,128]{1,0:T(8,128)S(1)}, f32[512,128]{1,0:T(8,128)S(1)}, u32[]{:S(2)}, u32[]{:S(2)}) collective-permute-start(f32[512,128]{1,0:T(8,128)S(1)} %fusion.80), channel_id=1, source_target_pairs={{1,0},{2,1},{3,2},{4,3},{5,4},{6,5},{7,6},{8,7},{9,8},{10,9},{11,1... | collective-permute-start | bytes 786440 | tf_op jit(solution)/shard_map/ppermute | solution.py:12
  81.5 0.6 fusion.81
  82.1 1.9 %collective-permute-start.6 = (f32[512,128]{1,0:T(8,128)S(1)}, f32[512,128]{1,0:T(8,128)S(1)}, u32[]{:S(2)}, u32[]{:S(2)}) collective-permute-start(f32[512,128]{1,0:T(8,128)S(1)} %fusion.81), channel_id=1, source_target_pairs={{0,1},{1,2},{2,3},{3,4},{4,5},{5,6},{6,7},{7,8},{8,9},{9,10},{10,1... | collective-permute-start | bytes 786440 | tf_op jit(solution)/shard_map/ppermute | solution.py:12
  84.0 21.4 %collective-permute-done.8 = f32[512,128]{1,0:T(8,128)S(1)} collective-permute-done((f32[512,128]{1,0:T(8,128)S(1)}, f32[512,128]{1,0:T(8,128)S(1)}, u32[]{:S(2)}, u32[]{:S(2)}) %collective-permute-start.8) | collective-permute-done | bytes 262176 | tf_op jit(solution)/shard_map/ppermute | solution.py:12
  105.4 0.6 fusion.99
  106.0 5.6 %collective-permute-start.9 = (f32[512,128]{1,0:T(8,128)S(1)}, f32[512,128]{1,0:T(8,128)S(1)}, u32[]{:S(2)}, u32[]{:S(2)}) collective-permute-start(f32[512,128]{1,0:T(8,128)S(1)} %fusion.99), channel_id=1, source_target_pairs={{1,0},{2,1},{3,2},{4,3},{5,4},{6,5},{7,6},{8,7},{9,8},{10,9},{11,1... | collective-permute-start | bytes 786440 | tf_op jit(solution)/shard_map/ppermute | solution.py:12
  111.6 0.0 collective-permute-done.10
  111.6 1.0 fusion.100
  112.7 1.9 %collective-permute-start.11 = (f32[512,512]{1,0:T(8,128)S(1)}, f32[512,512]{1,0:T(8,128)S(1)}, u32[]{:S(2)}, u32[]{:S(2)}) collective-permute-start(f32[512,512]{1,0:T(8,128)S(1)} %fusion.100), channel_id=1, source_target_pairs={{0,1},{1,2},{2,3},{3,4},{4,5},{5,6},{6,7},{7,8},{8,9},{9,10},{10,1... | collective-permute-start | bytes 3145736 | tf_op jit(solution)/shard_map/ppermute | solution.py:12
  114.6 1.0 fusion.101
  115.7 5.1 %collective-permute-start.13 = (f32[512,512]{1,0:T(8,128)S(1)}, f32[512,512]{1,0:T(8,128)S(1)}, u32[]{:S(2)}, u32[]{:S(2)}) collective-permute-start(f32[512,512]{1,0:T(8,128)S(1)} %fusion.101), channel_id=1, source_target_pairs={{1,0},{2,1},{3,2},{4,3},{5,4},{6,5},{7,6},{8,7},{9,8},{10,9},{11,1... | collective-permute-start | bytes 3145736 | tf_op jit(solution)/shard_map/ppermute | solution.py:12
  120.7 0.6 fusion.98
  121.3 1.9 %collective-permute-start.7 = (f32[512,128]{1,0:T(8,128)S(1)}, f32[512,128]{1,0:T(8,128)S(1)}, u32[]{:S(2)}, u32[]{:S(2)}) collective-permute-start(f32[512,128]{1,0:T(8,128)S(1)} %fusion.98), channel_id=1, source_target_pairs={{0,1},{1,2},{2,3},{3,4},{4,5},{5,6},{6,7},{7,8},{8,9},{9,10},{10,1... | collective-permute-start | bytes 786440 | tf_op jit(solution)/shard_map/ppermute | solution.py:12
  123.3 0.6 fusion.11
  123.9 23.0 %collective-permute-done.7 = f32[512,128]{1,0:T(8,128)S(1)} collective-permute-done((f32[512,128]{1,0:T(8,128)S(1)}, f32[512,128]{1,0:T(8,128)S(1)}, u32[]{:S(2)}, u32[]{:S(2)}) %collective-permute-start.7) | collective-permute-done | bytes 262176 | tf_op jit(solution)/shard_map/ppermute | solution.py:12
  146.8 0.6 fusion.4
  147.4 0.0 collective-permute-done.11
  147.5 1.0 fusion.24
  148.5 1.0 fusion.7
  149.6 0.2 copy-done.8
  149.7 1.0 fusion.102
  150.8 0.2 copy-done.10
  151.0 1.7 %select_reduce_fusion = (f32[]{:T(128)}, f32[512,512]{1,0:T(8,128)S(1)}) fusion(f32[512,512]{1,0:T(8,128)S(1)} %fusion.102, f32[512,512]{1,0:T(8,128)S(1)} %copy-done.6, f32[512,512]{1,0:T(8,128)S(1)} %fusion.24, f32[512,512]{1,0:T(8,128)S(1)} %copy-done.10), kind=kOutput, calls=%fused_computation.46 | convolution fusion | flops 806617088 | bytes 5242884 | tf_op jit(solution)/shard_map/dot_general | solution.py:16
  153.4 0.6 fusion.48
  154.0 0.6 convolution_add_fusion.3
  154.6 1.3 multiply_bitcast_fusion
  (29 shorter events, 0.1 us)
Async XLA Ops:
  0.0 9.9 %copy-start.4 = (f32[1,512,512]{2,1,0:T(8,128)S(1)}, f32[1,512,512]{2,1,0:T(8,128)}, u32[]{:S(2)}) copy-start(f32[1,512,512]{2,1,0:T(8,128)} %param.5) | copy-start | bytes 3145732
  0.0 16.8 %collective-permute-start.2 = (f32[512,128]{1,0:T(8,128)}, f32[512,128]{1,0:T(8,128)S(1)}, u32[]{:S(2)}, u32[]{:S(2)}) collective-permute-start(f32[512,128]{1,0:T(8,128)} %bitcast.86), channel_id=1, source_target_pairs={{1,0},{2,1},{3,2},{4,3},{5,4},{6,5},{7,6},{8,7},{9,8},{10,9},{11,1... | collective-permute-start | bytes 786440 | tf_op jit(solution)/shard_map/ppermute | solution.py:12
  5.3 9.9 %collective-permute-start = (f32[512,128]{1,0:T(8,128)}, f32[512,128]{1,0:T(8,128)}, u32[]{:S(2)}, u32[]{:S(2)}) collective-permute-start(f32[512,128]{1,0:T(8,128)} %bitcast.87), channel_id=1, source_target_pairs={{0,1},{1,2},{2,3},{3,4},{4,5},{5,6},{6,7},{7,8},{8,9},{9,10},{10,1... | collective-permute-start | bytes 786440 | tf_op jit(solution)/shard_map/ppermute | solution.py:12
  10.9 1.2 copy-start.1
  12.2 1.2 copy-start
  13.4 14.9 %copy-start.2 = (f32[512,512]{1,0:T(8,128)}, f32[512,512]{1,0:T(8,128)S(1)}, u32[]{:S(2)}) copy-start(f32[512,512]{1,0:T(8,128)S(1)} %fusion.17) | copy-start | bytes 3145732
  13.4 1.1 copy-start.15
  17.6 12.8 %collective-permute-start.1 = (f32[512,256]{0,1:T(8,128)S(1)}, f32[512,256]{0,1:T(8,128)S(1)}, u32[]{:S(2)}, u32[]{:S(2)}) collective-permute-start(f32[512,256]{0,1:T(8,128)S(1)} %get-tuple-element.5), channel_id=1, source_target_pairs={{0,1},{1,2},{2,3},{3,4},{4,5},{5,6},{6,7},{7,8},{8,9},{9,10},{10,1... | collective-permute-start | bytes 1572872 | tf_op jit(solution)/shard_map/ppermute | solution.py:12
  19.5 27.8 %collective-permute-start.3 = (f32[512,256]{0,1:T(8,128)S(1)}, f32[512,256]{0,1:T(8,128)S(1)}, u32[]{:S(2)}, u32[]{:S(2)}) collective-permute-start(f32[512,256]{0,1:T(8,128)S(1)} %get-tuple-element.6), channel_id=1, source_target_pairs={{1,0},{2,1},{3,2},{4,3},{5,4},{6,5},{7,6},{8,7},{9,8},{10,9},{11,1... | collective-permute-start | bytes 1572872 | tf_op jit(solution)/shard_map/ppermute | solution.py:12
  24.4 34.2 %collective-permute-start.5 = (f32[512,512]{1,0:T(8,128)S(1)}, f32[512,512]{1,0:T(8,128)S(1)}, u32[]{:S(2)}, u32[]{:S(2)}) collective-permute-start(f32[512,512]{1,0:T(8,128)S(1)} %fusion.30), channel_id=1, source_target_pairs={{1,0},{2,1},{3,2},{4,3},{5,4},{6,5},{7,6},{8,7},{9,8},{10,9},{11,1... | collective-permute-start | bytes 3145736 | tf_op jit(solution)/shard_map/ppermute | solution.py:12
  28.3 32.1 %collective-permute-start.4 = (f32[512,512]{1,0:T(8,128)S(1)}, f32[512,512]{1,0:T(8,128)S(1)}, u32[]{:S(2)}, u32[]{:S(2)}) collective-permute-start(f32[512,512]{1,0:T(8,128)S(1)} %fusion.17), channel_id=1, source_target_pairs={{0,1},{1,2},{2,3},{3,4},{4,5},{5,6},{6,7},{7,8},{8,9},{9,10},{10,1... | collective-permute-start | bytes 3145736 | tf_op jit(solution)/shard_map/ppermute | solution.py:12
  31.1 16.9 %copy-start.11 = (f32[512,256]{1,0:T(8,128)}, f32[512,256]{1,0:T(8,128)S(1)}, u32[]{:S(2)}) copy-start(f32[512,256]{1,0:T(8,128)S(1)} %fusion.28) | copy-start | bytes 1572868
  48.0 0.8 copy-start.13
  48.8 11.7 %copy-start.5 = (f32[1,512,512]{2,1,0:T(8,128)S(1)}, f32[1,512,512]{2,1,0:T(8,128)}, u32[]{:S(2)}) copy-start(f32[1,512,512]{2,1,0:T(8,128)} %param.5) | copy-start | bytes 3145732
  58.6 1.1 copy-start.7
  60.5 2.7 %copy-start.9 = (f32[512,512]{1,0:T(8,128)}, f32[512,512]{1,0:T(8,128)S(1)}, u32[]{:S(2)}) copy-start(f32[512,512]{1,0:T(8,128)S(1)} %collective-permute-done.4) | copy-start | bytes 3145732
  63.8 2.7 %copy-start.6 = (f32[512,512]{1,0:T(8,128)S(1)}, f32[512,512]{1,0:T(8,128)}, u32[]{:S(2)}) copy-start(f32[512,512]{1,0:T(8,128)} %get-tuple-element.8) | copy-start | bytes 3145732
  68.7 8.1 %copy-start.14 = (f32[512,256]{1,0:T(8,128)S(1)}, f32[512,256]{1,0:T(8,128)}, u32[]{:S(2)}) copy-start(f32[512,256]{1,0:T(8,128)} %copy-done.13) | copy-start | bytes 1572868
  68.7 42.9 %collective-permute-start.10 = (f32[512,512]{1,0:T(8,128)S(1)}, f32[512,512]{1,0:T(8,128)S(1)}, u32[]{:S(2)}, u32[]{:S(2)}) collective-permute-start(f32[512,512]{1,0:T(8,128)S(1)} %fusion.9), channel_id=1, source_target_pairs={{0,1},{1,2},{2,3},{3,4},{4,5},{5,6},{6,7},{7,8},{8,9},{9,10},{10,1... | collective-permute-start | bytes 3145736 | tf_op jit(solution)/shard_map/ppermute | solution.py:12
  72.7 8.7 %copy-start.12 = (f32[512,256]{1,0:T(8,128)S(1)}, f32[512,256]{1,0:T(8,128)}, u32[]{:S(2)}) copy-start(f32[512,256]{1,0:T(8,128)} %copy-done.11) | copy-start | bytes 1572868
  72.7 41.9 %collective-permute-start.12 = (f32[512,512]{1,0:T(8,128)S(1)}, f32[512,512]{1,0:T(8,128)S(1)}, u32[]{:S(2)}, u32[]{:S(2)}) collective-permute-start(f32[512,512]{1,0:T(8,128)S(1)} %fusion.22), channel_id=1, source_target_pairs={{1,0},{2,1},{3,2},{4,3},{5,4},{6,5},{7,6},{8,7},{9,8},{10,9},{11,1... | collective-permute-start | bytes 3145736 | tf_op jit(solution)/shard_map/ppermute | solution.py:12
  77.4 28.0 %copy-start.3 = (f32[512,512]{1,0:T(8,128)S(1)}, f32[512,512]{1,0:T(8,128)}, u32[]{:S(2)}) copy-start(f32[512,512]{1,0:T(8,128)} %copy-done.2) | copy-start | bytes 3145732
  77.4 28.0 %collective-permute-start.8 = (f32[512,128]{1,0:T(8,128)S(1)}, f32[512,128]{1,0:T(8,128)S(1)}, u32[]{:S(2)}, u32[]{:S(2)}) collective-permute-start(f32[512,128]{1,0:T(8,128)S(1)} %fusion.80), channel_id=1, source_target_pairs={{1,0},{2,1},{3,2},{4,3},{5,4},{6,5},{7,6},{8,7},{9,8},{10,9},{11,1... | collective-permute-start | bytes 786440 | tf_op jit(solution)/shard_map/ppermute | solution.py:12
  82.1 38.7 %collective-permute-start.6 = (f32[512,128]{1,0:T(8,128)S(1)}, f32[512,128]{1,0:T(8,128)S(1)}, u32[]{:S(2)}, u32[]{:S(2)}) collective-permute-start(f32[512,128]{1,0:T(8,128)S(1)} %fusion.81), channel_id=1, source_target_pairs={{0,1},{1,2},{2,3},{3,4},{4,5},{5,6},{6,7},{7,8},{8,9},{9,10},{10,1... | collective-permute-start | bytes 786440 | tf_op jit(solution)/shard_map/ppermute | solution.py:12
  106.0 17.3 %collective-permute-start.9 = (f32[512,128]{1,0:T(8,128)S(1)}, f32[512,128]{1,0:T(8,128)S(1)}, u32[]{:S(2)}, u32[]{:S(2)}) collective-permute-start(f32[512,128]{1,0:T(8,128)S(1)} %fusion.99), channel_id=1, source_target_pairs={{1,0},{2,1},{3,2},{4,3},{5,4},{6,5},{7,6},{8,7},{9,8},{10,9},{11,1... | collective-permute-start | bytes 786440 | tf_op jit(solution)/shard_map/ppermute | solution.py:12
  112.7 34.8 %collective-permute-start.11 = (f32[512,512]{1,0:T(8,128)S(1)}, f32[512,512]{1,0:T(8,128)S(1)}, u32[]{:S(2)}, u32[]{:S(2)}) collective-permute-start(f32[512,512]{1,0:T(8,128)S(1)} %fusion.100), channel_id=1, source_target_pairs={{0,1},{1,2},{2,3},{3,4},{4,5},{5,6},{6,7},{7,8},{8,9},{9,10},{10,1... | collective-permute-start | bytes 3145736 | tf_op jit(solution)/shard_map/ppermute | solution.py:12
  115.7 32.9 %collective-permute-start.13 = (f32[512,512]{1,0:T(8,128)S(1)}, f32[512,512]{1,0:T(8,128)S(1)}, u32[]{:S(2)}, u32[]{:S(2)}) collective-permute-start(f32[512,512]{1,0:T(8,128)S(1)} %fusion.101), channel_id=1, source_target_pairs={{1,0},{2,1},{3,2},{4,3},{5,4},{6,5},{7,6},{8,7},{9,8},{10,9},{11,1... | collective-permute-start | bytes 3145736 | tf_op jit(solution)/shard_map/ppermute | solution.py:12
  121.3 25.5 %collective-permute-start.7 = (f32[512,128]{1,0:T(8,128)S(1)}, f32[512,128]{1,0:T(8,128)S(1)}, u32[]{:S(2)}, u32[]{:S(2)}) collective-permute-start(f32[512,128]{1,0:T(8,128)S(1)} %fusion.98), channel_id=1, source_target_pairs={{0,1},{1,2},{2,3},{3,4},{4,5},{5,6},{6,7},{7,8},{8,9},{9,10},{10,1... | collective-permute-start | bytes 786440 | tf_op jit(solution)/shard_map/ppermute | solution.py:12
  148.5 1.2 copy-start.8
  149.7 1.2 copy-start.10
where the time goes:
time: 157 us; the launch traced here: 156 us
  waiting for transfers between devices  71.3 us (45%)
  starting transfers between devices  47.5 us (30%)
  matrix products  30.9 us (20%)
  between operations  2.61 us (2%)
  other arithmetic  2.06 us (1%)
    ppermute x14, waiting for transfers between devices, shifted(): lax.ppermute(value, AXES, [(source, source + steps) for source in range(i...  71.3 us
    ppermute x14, starting transfers between devices, shifted(): lax.ppermute(value, AXES, [(source, source + steps) for source in range(i...  47.5 us
    dot_general x30, matrix products, multiply(): jnp.dot(left, right, precision=lax.Precision.HIGH, preferred_element_type...  30.9 us
  transfers between devices with their start and end apart: 14, of which 5 were waited for; matrix products, arithmetic and copies ran while one was open for 12% of the time, Pallas kernels for 0%

commit v1 on v0

v1 whole, which is shorter than its diff:
```python
import jax
import jax.numpy as jnp
from jax import lax
from jax.experimental import pallas as pl
from jax.experimental.pallas import tpu as pltpu
from jax.sharding import PartitionSpec as P

AXES = ("row", "col")

VECTOR_WEIGHT = 10**10
PASS_WEIGHT = 10**10
MIDDLE_WEIGHT = 10**10

VMEM_LIMIT = 24 * 1024 * 1024
FIRST_LIMIT = 60 * 1024 * 1024


def shifted(value, steps):
    count = lax.axis_size(AXES)
    initial, last = (max(0, -steps), min(count, count - steps))
    return lax.ppermute(value, AXES, [(source, source + steps) for source in range(initial, last)])


def split(value):
    high = value.astype(jnp.bfloat16)
    return high, (value - high.astype(jnp.float32)).astype(jnp.bfloat16)


def multiply(left, right):
    (lh, ll), (rh, rl) = left, right
    cols = rh.shape[1]
    if cols <= 128:
        both = dot(lh, jnp.concatenate([rh, rl], axis=1))
        return both[:, :cols] + (both[:, cols:] + dot(ll, rh))
    return dot(lh, rh) + (dot(lh, rl) + dot(ll, rh))


def dot(left, right):
    return jnp.dot(left, right, preferred_element_type=jnp.float32)


def on_diagonal(order):
    rows = lax.broadcasted_iota(jnp.int32, (order, order), 0)
    return rows == lax.broadcasted_iota(jnp.int32, (order, order), 1)


def residual(matrix):
    order = matrix.shape[-1]
    same = on_diagonal(order)
    picked = jnp.where(same, matrix, 0.0)
    total = jnp.sum(jnp.sum(picked, axis=0, keepdims=True), axis=1, keepdims=True)
    scale = order / total
    return jnp.where(same, 1.0, 0.0) - matrix * scale, scale


def invert(matrix):
    rest, scale = residual(matrix)
    halves = split(rest)
    square = multiply(halves, halves)
    cube = multiply(halves, split(square))
    eye = jnp.where(on_diagonal(matrix.shape[-1]), 1.0, 0.0)
    return (eye + (rest + (square + cube))) * scale


def first_kernel(diag, low, up, rhs, scaled_up, scaled_low, scaled_rhs, diag_v, low_v, up_v, rhs_v, sems):
    pairs = ((diag, diag_v), (up, up_v), (low, low_v), (rhs, rhs_v))
    copies = [pltpu.make_async_copy(*pair, sems.at[place]) for place, pair in enumerate(pairs)]
    for copy in copies:
        copy.start()
    copies[0].wait()
    pivot = split(invert(diag_v[...]))
    copies[1].wait()
    scaled_up[...] = multiply(pivot, split(up_v[...]))
    copies[2].wait()
    scaled_low[...] = multiply(pivot, split(low_v[...]))
    copies[3].wait()
    scaled_rhs[...] = multiply(pivot, split(rhs_v[...]))


def vector_kernel(scaled_up, scaled_low, scaled_rhs, guess_l, guess_r, to_up, to_down):
    cols = scaled_rhs.shape[1]
    value = scaled_rhs[...]
    to_up[:, :cols] = value
    to_down[:, :cols] = value
    to_up[:, cols:] = multiply(split(scaled_low[...]), split(guess_l[...]))
    to_down[:, cols:] = multiply(split(scaled_up[...]), split(guess_r[...]))


def second_kernel(diag, low, up, up_l, low_r, diag1, pivot1, to_up, to_down):
    low_halves, up_halves = split(low[...]), split(up[...])
    value = diag[...] - multiply(low_halves, split(up_l[...])) - multiply(up_halves, split(low_r[...]))
    diag1[...] = value
    pivot = invert(value)
    pivot1[...] = pivot
    halves = split(pivot)
    to_up[...] = multiply(halves, up_halves)
    to_down[...] = multiply(halves, low_halves)


def middle_kernel(low, up, rhs, pivot1, vec_l, vec_r, rhs1, to_up, to_down):
    cols = rhs.shape[1]
    lv = multiply(split(low[...]), split(vec_l[...]))
    uv = multiply(split(up[...]), split(vec_r[...]))
    value = rhs[...] - lv[:, :cols] - uv[:, :cols]
    rhs1[...] = value
    pivot = split(pivot1[...])
    to_up[...] = multiply(pivot, split(value + lv[:, cols:]))
    to_down[...] = multiply(pivot, split(value + uv[:, cols:]))


def pair_kernel(left, right, out):
    out[...] = multiply(split(left[...]), split(right[...]))


def two_pairs_kernel(left_a, right_a, left_b, right_b, out_a, out_b):
    out_a[...] = multiply(split(left_a[...]), split(right_a[...]))
    out_b[...] = multiply(split(left_b[...]), split(right_b[...]))


def inner_kernel(rhs1, low, up, d_l, d_r, out):
    out[...] = rhs1[...] + multiply(split(low[...]), split(d_l[...])) + multiply(split(up[...]), split(d_r[...]))


def triple(first, second, third):
    return multiply(split(multiply(split(first), split(second))), split(third))


def before_last_kernel(base, first, second, third, out):
    out[...] = base[...] - triple(first[...], second[...], third[...])


def last_kernel(base, first, second, third, inner_ref, out):
    rest, scale = residual(base[...] - triple(first[...], second[...], third[...]))
    halves = split(rest)
    inner = inner_ref[...]
    part = inner + multiply(halves, split(multiply(halves, split(inner))))
    out[...] = (part + multiply(halves, split(part))) * scale


def call(kernel, outs, *args, weight=0, limit=VMEM_LIMIT, **options):
    in_vmem = pl.BlockSpec(memory_space=pltpu.VMEM)
    options = {"in_specs": [in_vmem] * len(args)} | options
    return pl.pallas_call(
        kernel,
        out_shape=[jax.ShapeDtypeStruct(shape, jnp.float32) for shape in outs],
        out_specs=[in_vmem] * len(outs),
        compiler_params=pltpu.CompilerParams(vmem_limit_bytes=limit),
        cost_estimate=pl.CostEstimate(flops=weight, bytes_accessed=0, transcendentals=0),
        **options,
    )(*args)


def body(diagonal, lower, upper, right_side, guess):
    diag, low, up, rhs = diagonal[0], lower[0], upper[0], right_side[0]
    square, tall = diag.shape, rhs.shape
    wide = (tall[0], 2 * tall[1])
    guess_l = shifted(guess[0], 1)
    guess_r = shifted(guess[0], -1)
    scaled_up, scaled_low, scaled_rhs = call(
        first_kernel,
        (square, square, tall),
        *(diag, low, up, rhs),
        limit=FIRST_LIMIT,
        in_specs=[pl.BlockSpec(memory_space=pl.ANY)] * 4,
        scratch_shapes=[pltpu.VMEM(shape, jnp.float32) for shape in (square, square, square, tall)]
        + [pltpu.SemaphoreType.DMA((4,))],
    )
    up_l = shifted(scaled_up, 1)
    low_r = shifted(scaled_low, -1)
    to_up, to_down = call(
        vector_kernel, (wide, wide), scaled_up, scaled_low, scaled_rhs, guess_l, guess_r, weight=VECTOR_WEIGHT
    )
    vec_l = shifted(to_up, 1)
    vec_r = shifted(to_down, -1)
    diag1, pivot1, next_up, next_down = call(second_kernel, (square,) * 4, diag, low, up, up_l, low_r)
    next_l = shifted(next_up, 1)
    next_r = shifted(next_down, -1)
    rhs1, w_up, w_down = call(
        middle_kernel, (tall,) * 3, low, up, rhs, pivot1, vec_l, vec_r, weight=MIDDLE_WEIGHT
    )
    w_l = shifted(w_up, 1)
    w_r = shifted(w_down, -1)
    scaled_low, scaled_up, _, _ = lax.optimization_barrier((scaled_low, scaled_up, w_up, w_down))
    (pass_up,) = call(pair_kernel, (square,), scaled_low, next_l)
    (pass_down,) = call(pair_kernel, (square,), scaled_up, next_r)
    pass_l = shifted(pass_up, 1)
    pass_r = shifted(pass_down, -1)
    w_l, w_r, _, _ = lax.optimization_barrier((w_l, w_r, pass_up, pass_down))
    d_up, d_down = call(two_pairs_kernel, (tall, tall), scaled_low, w_l, scaled_up, w_r, weight=PASS_WEIGHT)
    d_l = shifted(d_up, 1)
    d_r = shifted(d_down, -1)
    (inner,) = call(inner_kernel, (tall,), rhs1, low, up, d_l, d_r)
    (part2,) = call(before_last_kernel, (square,), diag1, low, pass_l, up_l)
    part2, inner = lax.optimization_barrier((part2, inner))
    (out,) = call(last_kernel, (tall,), part2, up, pass_r, low_r, inner)
    return out[None]


def solution(mesh):
    spec = P(AXES, None, None)
    return jax.shard_map(
        body,
        mesh=mesh,
        in_specs=(spec,) * 5,
        out_specs=spec,
        check_vma=False,
    )
```

time: 157 us -> 132 us (0.84)
  the two profiles are of different devices: /device:TPU:129 before, /device:TPU:161 now
where the time goes in v1:
time: 132 us
  waiting for transfers between devices  54.9 us (42%)
  starting transfers between devices  49 us (37%)
  Pallas kernels  24 us (18%)
  local copies, waits for them, and re-layouts  3.42 us (3%)
    ppermute x14, waiting for transfers between devices, shifted(): lax.ppermute(value, AXES, [(source, source + steps) for source in range(i...  54.9 us
    ppermute x14, starting transfers between devices, shifted(): lax.ppermute(value, AXES, [(source, source + steps) for source in range(i...  49 us
    pallas_call x10, Pallas kernels, call(): pl.pallas_call(kernel, out_shape=[jax.ShapeDtypeStruct(shape, jnp.float32...  24 us
    unnamed x18, local copies, waits for them, and re-layouts  3.42 us
  transfers between devices with their start and end apart: 14, of which 5 were waited for; matrix products, arithmetic and copies ran while one was open for 0% of the time, Pallas kernels for 15%

profile of v1, /device:TPU:161, one launch (start us, length us, event | category | flops | bytes accessed | tf_op | source)
XLA Modules:
  0.0 131.6 jit_solution(6686862039644388744)
XLA Ops:
  0.0 5.2 %collective-permute-start.3 = (f32[512,128]{1,0:T(8,128)}, f32[512,128]{1,0:T(8,128)S(1)}, u32[]{:S(2)}, u32[]{:S(2)}) collective-permute-start(f32[512,128]{1,0:T(8,128)} %bitcast.20), channel_id=1, source_target_pairs={{1,0},{2,1},{3,2},{4,3},{5,4},{6,5},{7,6},{8,7},{9,8},{10,9},{11,1... | collective-permute-start | bytes 786440 | tf_op jit(solution)/shard_map/ppermute | solution.py:21
  5.2 1.9 %collective-permute-start.2 = (f32[512,128]{1,0:T(8,128)}, f32[512,128]{1,0:T(8,128)S(1)}, u32[]{:S(2)}, u32[]{:S(2)}) collective-permute-start(f32[512,128]{1,0:T(8,128)} %bitcast.21), channel_id=1, source_target_pairs={{0,1},{1,2},{2,3},{3,4},{4,5},{5,6},{6,7},{7,8},{8,9},{9,10},{10,1... | collective-permute-start | bytes 786440 | tf_op jit(solution)/shard_map/ppermute | solution.py:21
  7.1 6.8 %shard_map.55 = (f32[512,512]{1,0:T(8,128)}, f32[512,512]{1,0:T(8,128)}, f32[512,128]{1,0:T(8,128)}) custom-call(f32[512,512]{1,0:T(8,128)} %bitcast.16, f32[512,512]{1,0:T(8,128)} %bitcast.6, f32[512,512]{1,0:T(8,128)} %bitcast.11, f32[512,128]{1,0:T(8,128)} %bitcast.18), custom_call_target="tpu_custom_call" | custom-call | tf_op jit(solution)/shard_map/pallas_call | solution.py:143
  14.0 1.9 %collective-permute-start = (f32[512,512]{1,0:T(8,128)}, f32[512,512]{1,0:T(8,128)S(1)}, u32[]{:S(2)}, u32[]{:S(2)}) collective-permute-start(f32[512,512]{1,0:T(8,128)} %get-tuple-element.37.scaled_up.left.left_b), channel_id=1, source_target_pairs={{0,1},{1,2},{2,3},{3,4},{4,5},{5,6},{6,7},{7,8},{8,9},{9,10},{10,1... | collective-permute-start | bytes 3145736 | tf_op jit(solution)/shard_map/ppermute | solution.py:21
  15.9 4.9 %collective-permute-start.1 = (f32[512,512]{1,0:T(8,128)}, f32[512,512]{1,0:T(8,128)S(1)}, u32[]{:S(2)}, u32[]{:S(2)}) collective-permute-start(f32[512,512]{1,0:T(8,128)} %get-tuple-element.34.scaled_low.left.left_a), channel_id=1, source_target_pairs={{1,0},{2,1},{3,2},{4,3},{5,4},{6,5},{7,6},{8,7},{9,8},{10,9},{11,1... | collective-permute-start | bytes 3145736 | tf_op jit(solution)/shard_map/ppermute | solution.py:21
  20.8 0.0 collective-permute-done.3.guess_r
  20.8 0.0 collective-permute-done.2.guess_l
  20.8 0.0 copy-start.3
  20.8 1.2 copy-done.3
  22.0 0.0 copy-start.5
  22.0 1.2 copy-done.5
  23.2 0.0 copy-start.8
  23.2 0.9 copy-done.8
  24.2 0.0 copy-start
  24.2 0.0 copy-start.1
  24.2 0.0 copy-start.2
  24.2 0.7 shard_map.57
  24.9 2.1 %collective-permute-start.4 = (f32[512,256]{1,0:T(8,128)S(1)}, f32[512,256]{1,0:T(8,128)S(1)}, u32[]{:S(2)}, u32[]{:S(2)}) collective-permute-start(f32[512,256]{1,0:T(8,128)S(1)} %get-tuple-element.30), channel_id=1, source_target_pairs={{0,1},{1,2},{2,3},{3,4},{4,5},{5,6},{6,7},{7,8},{8,9},{9,10},{10,1... | collective-permute-start | bytes 1572872 | tf_op jit(solution)/shard_map/ppermute | solution.py:21
  27.0 0.0 copy-start.7
  27.0 5.0 %collective-permute-start.5 = (f32[512,256]{1,0:T(8,128)S(1)}, f32[512,256]{1,0:T(8,128)S(1)}, u32[]{:S(2)}, u32[]{:S(2)}) collective-permute-start(f32[512,256]{1,0:T(8,128)S(1)} %get-tuple-element.31), channel_id=1, source_target_pairs={{1,0},{2,1},{3,2},{4,3},{5,4},{6,5},{7,6},{8,7},{9,8},{10,9},{11,1... | collective-permute-start | bytes 1572872 | tf_op jit(solution)/shard_map/ppermute | solution.py:21
  32.0 16.4 %collective-permute-done.up_l.third = f32[512,512]{1,0:T(8,128)S(1)} collective-permute-done((f32[512,512]{1,0:T(8,128)}, f32[512,512]{1,0:T(8,128)S(1)}, u32[]{:S(2)}, u32[]{:S(2)}) %collective-permute-start) | collective-permute-done | bytes 1048608 | tf_op jit(solution)/shard_map/ppermute | solution.py:21
  48.4 1.3 collective-permute-done.1.low_r.third
  49.6 0.0 copy-done
  49.7 0.0 copy-done.1
  49.7 0.0 copy-done.2
  49.7 5.6 %shard_map.56 = (f32[512,512]{1,0:T(8,128)S(1)}, f32[512,512]{1,0:T(8,128)S(1)}, f32[512,512]{1,0:T(8,128)S(1)}, f32[512,512]{1,0:T(8,128)S(1)}) custom-call(f32[512,512]{1,0:T(8,128)S(1)} %bitcast.17, f32[512,512]{1,0:T(8,128)S(1)} %bitcast.7, f32[512,512]{1,0:T(8,128)S(1)} %bitcast.12, f32[512,512]{1,0:T(8,128)S(1)} %collective-permute-done.up_l.third, ...), custom_call_target="tpu_custom_call" | custom-call | tf_op jit(solution)/shard_map/pallas_call | solution.py:143
  55.3 1.9 %collective-permute-start.6 = (f32[512,512]{1,0:T(8,128)S(1)}, f32[512,512]{1,0:T(8,128)S(1)}, u32[]{:S(2)}, u32[]{:S(2)}) collective-permute-start(f32[512,512]{1,0:T(8,128)S(1)} %get-tuple-element.35), channel_id=1, source_target_pairs={{0,1},{1,2},{2,3},{3,4},{4,5},{5,6},{6,7},{7,8},{8,9},{9,10},{10,1... | collective-permute-start | bytes 3145736 | tf_op jit(solution)/shard_map/ppermute | solution.py:21
  57.2 5.5 %collective-permute-start.10 = (f32[512,512]{1,0:T(8,128)S(1)}, f32[512,512]{1,0:T(8,128)S(1)}, u32[]{:S(2)}, u32[]{:S(2)}) collective-permute-start(f32[512,512]{1,0:T(8,128)S(1)} %get-tuple-element.38), channel_id=1, source_target_pairs={{1,0},{2,1},{3,2},{4,3},{5,4},{6,5},{7,6},{8,7},{9,8},{10,9},{11,1... | collective-permute-start | bytes 3145736 | tf_op jit(solution)/shard_map/ppermute | solution.py:21
  62.7 0.0 collective-permute-done.4.vec_l
  62.7 0.0 collective-permute-done.5.vec_r
  62.7 0.0 copy-done.7
  62.7 0.0 copy-start.6
  62.8 1.6 %shard_map.58 = (f32[512,128]{1,0:T(8,128)S(1)}, f32[512,128]{1,0:T(8,128)S(1)}, f32[512,128]{1,0:T(8,128)S(1)}) custom-call(f32[512,512]{1,0:T(8,128)S(1)} %bitcast.8, f32[512,512]{1,0:T(8,128)S(1)} %bitcast.13, f32[512,128]{1,0:T(8,128)S(1)} %bitcast.19, f32[512,512]{1,0:T(8,128)S(1)} %get-tuple-element.28.pivot1, ...), custom_call_target="tpu_custom_call" | custom-call | flops 10000000000 | tf_op jit(solution)/shard_map/pallas_call | solution.py:143
  64.4 1.9 %collective-permute-start.8 = (f32[512,128]{1,0:T(8,128)S(1)}, f32[512,128]{1,0:T(8,128)S(1)}, u32[]{:S(2)}, u32[]{:S(2)}) collective-permute-start(f32[512,128]{1,0:T(8,128)S(1)} %get-tuple-element.32), channel_id=1, source_target_pairs={{0,1},{1,2},{2,3},{3,4},{4,5},{5,6},{6,7},{7,8},{8,9},{9,10},{10,1... | collective-permute-start | bytes 786440 | tf_op jit(solution)/shard_map/ppermute | solution.py:21
  66.3 0.0 copy-start.4
  66.3 5.0 %collective-permute-start.9 = (f32[512,128]{1,0:T(8,128)S(1)}, f32[512,128]{1,0:T(8,128)S(1)}, u32[]{:S(2)}, u32[]{:S(2)}) collective-permute-start(f32[512,128]{1,0:T(8,128)S(1)} %get-tuple-element.33), channel_id=1, source_target_pairs={{1,0},{2,1},{3,2},{4,3},{5,4},{6,5},{7,6},{8,7},{9,8},{10,9},{11,1... | collective-permute-start | bytes 786440 | tf_op jit(solution)/shard_map/ppermute | solution.py:21
  71.3 28.6 %collective-permute-done.6.right = f32[512,512]{1,0:T(8,128)S(1)} collective-permute-done((f32[512,512]{1,0:T(8,128)S(1)}, f32[512,512]{1,0:T(8,128)S(1)}, u32[]{:S(2)}, u32[]{:S(2)}) %collective-permute-start.6) | collective-permute-done | bytes 1048608 | tf_op jit(solution)/shard_map/ppermute | solution.py:21
  99.9 0.0 copy-done.6
  99.9 1.0 shard_map.59
  100.9 1.9 %collective-permute-start.7 = (f32[512,512]{1,0:T(8,128)S(1)}, f32[512,512]{1,0:T(8,128)S(1)}, u32[]{:S(2)}, u32[]{:S(2)}) collective-permute-start(f32[512,512]{1,0:T(8,128)S(1)} %shard_map.59), channel_id=1, source_target_pairs={{0,1},{1,2},{2,3},{3,4},{4,5},{5,6},{6,7},{7,8},{8,9},{9,10},{10,1... | collective-permute-start | bytes 3145736 | tf_op jit(solution)/shard_map/ppermute | solution.py:21
  102.9 0.0 collective-permute-done.10.right
  102.9 0.0 copy-done.4
  102.9 1.0 shard_map.61
  103.9 5.0 %collective-permute-start.13 = (f32[512,512]{1,0:T(8,128)S(1)}, f32[512,512]{1,0:T(8,128)S(1)}, u32[]{:S(2)}, u32[]{:S(2)}) collective-permute-start(f32[512,512]{1,0:T(8,128)S(1)} %shard_map.61), channel_id=1, source_target_pairs={{1,0},{2,1},{3,2},{4,3},{5,4},{6,5},{7,6},{8,7},{9,8},{10,9},{11,1... | collective-permute-start | bytes 3145736 | tf_op jit(solution)/shard_map/ppermute | solution.py:21
  108.9 0.0 collective-permute-done.8.right_a
  108.9 0.0 collective-permute-done.9.right_b
  108.9 0.7 shard_map.62
  109.7 1.9 %collective-permute-start.11 = (f32[512,128]{1,0:T(8,128)S(1)}, f32[512,128]{1,0:T(8,128)S(1)}, u32[]{:S(2)}, u32[]{:S(2)}) collective-permute-start(f32[512,128]{1,0:T(8,128)S(1)} %get-tuple-element.41), channel_id=1, source_target_pairs={{0,1},{1,2},{2,3},{3,4},{4,5},{5,6},{6,7},{7,8},{8,9},{9,10},{10,1... | collective-permute-start | bytes 786440 | tf_op jit(solution)/shard_map/ppermute | solution.py:21
  111.6 4.9 %collective-permute-start.12 = (f32[512,128]{1,0:T(8,128)S(1)}, f32[512,128]{1,0:T(8,128)S(1)}, u32[]{:S(2)}, u32[]{:S(2)}) collective-permute-start(f32[512,128]{1,0:T(8,128)S(1)} %get-tuple-element.42), channel_id=1, source_target_pairs={{1,0},{2,1},{3,2},{4,3},{5,4},{6,5},{7,6},{8,7},{9,8},{10,9},{11,1... | collective-permute-start | bytes 786440 | tf_op jit(solution)/shard_map/ppermute | solution.py:21
  116.4 4.6 %collective-permute-done.11.d_l = f32[512,128]{1,0:T(8,128)S(1)} collective-permute-done((f32[512,128]{1,0:T(8,128)S(1)}, f32[512,128]{1,0:T(8,128)S(1)}, u32[]{:S(2)}, u32[]{:S(2)}) %collective-permute-start.11) | collective-permute-done | bytes 262176 | tf_op jit(solution)/shard_map/ppermute | solution.py:21
  121.1 4.0 %collective-permute-done.12.d_r = f32[512,128]{1,0:T(8,128)S(1)} collective-permute-done((f32[512,128]{1,0:T(8,128)S(1)}, f32[512,128]{1,0:T(8,128)S(1)}, u32[]{:S(2)}, u32[]{:S(2)}) %collective-permute-start.12) | collective-permute-done | bytes 262176 | tf_op jit(solution)/shard_map/ppermute | solution.py:21
  125.0 0.7 shard_map.63.inner_ref
  125.8 0.0 collective-permute-done.7.second
  125.8 1.8 %shard_map.60.base = f32[512,512]{1,0:T(8,128)S(1)} custom-call(f32[512,512]{1,0:T(8,128)S(1)} %get-tuple-element.27.base, f32[512,512]{1,0:T(8,128)S(1)} %bitcast.10, f32[512,512]{1,0:T(8,128)S(1)} %collective-permute-done.7.second, f32[512,512]{1,0:T(8,128)S(1)} %collective-permute-done.up_l.third), custom_call_target="tpu_custom_call" | custom-call | tf_op jit(solution)/shard_map/pallas_call | solution.py:143
  127.6 0.0 collective-permute-done.13.second
  127.6 4.0 %shard_map.64 = f32[512,128]{1,0:T(8,128)} custom-call(f32[512,512]{1,0:T(8,128)S(1)} %shard_map.60.base, f32[512,512]{1,0:T(8,128)S(1)} %bitcast.15, f32[512,512]{1,0:T(8,128)S(1)} %collective-permute-done.13.second, f32[512,512]{1,0:T(8,128)S(1)} %collective-permute-done.1.low_r.third, f32[512,128]{1,0:T(8,128)S(1)} %shard_map.63.inner_ref), custom_call_target="tpu_custom_call" | custom-call | tf_op jit(solution)/shard_map/pallas_call | solution.py:143
Async XLA Ops:
  0.0 20.8 %collective-permute-start.3 = (f32[512,128]{1,0:T(8,128)}, f32[512,128]{1,0:T(8,128)S(1)}, u32[]{:S(2)}, u32[]{:S(2)}) collective-permute-start(f32[512,128]{1,0:T(8,128)} %bitcast.20), channel_id=1, source_target_pairs={{1,0},{2,1},{3,2},{4,3},{5,4},{6,5},{7,6},{8,7},{9,8},{10,9},{11,1... | collective-permute-start | bytes 786440 | tf_op jit(solution)/shard_map/ppermute | solution.py:21
  5.2 15.6 %collective-permute-start.2 = (f32[512,128]{1,0:T(8,128)}, f32[512,128]{1,0:T(8,128)S(1)}, u32[]{:S(2)}, u32[]{:S(2)}) collective-permute-start(f32[512,128]{1,0:T(8,128)} %bitcast.21), channel_id=1, source_target_pairs={{0,1},{1,2},{2,3},{3,4},{4,5},{5,6},{6,7},{7,8},{8,9},{9,10},{10,1... | collective-permute-start | bytes 786440 | tf_op jit(solution)/shard_map/ppermute | solution.py:21
  14.0 34.4 %collective-permute-start = (f32[512,512]{1,0:T(8,128)}, f32[512,512]{1,0:T(8,128)S(1)}, u32[]{:S(2)}, u32[]{:S(2)}) collective-permute-start(f32[512,512]{1,0:T(8,128)} %get-tuple-element.37.scaled_up.left.left_b), channel_id=1, source_target_pairs={{0,1},{1,2},{2,3},{3,4},{4,5},{5,6},{6,7},{7,8},{8,9},{9,10},{10,1... | collective-permute-start | bytes 3145736 | tf_op jit(solution)/shard_map/ppermute | solution.py:21
  15.9 33.8 %collective-permute-start.1 = (f32[512,512]{1,0:T(8,128)}, f32[512,512]{1,0:T(8,128)S(1)}, u32[]{:S(2)}, u32[]{:S(2)}) collective-permute-start(f32[512,512]{1,0:T(8,128)} %get-tuple-element.34.scaled_low.left.left_a), channel_id=1, source_target_pairs={{1,0},{2,1},{3,2},{4,3},{5,4},{6,5},{7,6},{8,7},{9,8},{10,9},{11,1... | collective-permute-start | bytes 3145736 | tf_op jit(solution)/shard_map/ppermute | solution.py:21
  20.8 1.2 copy-start.3
  22.0 1.2 copy-start.5
  23.2 0.9 copy-start.8
  24.2 25.5 %copy-start = (f32[1,512,512]{2,1,0:T(8,128)S(1)}, f32[1,512,512]{2,1,0:T(8,128)}, u32[]{:S(2)}) copy-start(f32[1,512,512]{2,1,0:T(8,128)} %param.6) | copy-start | bytes 3145732
  24.2 25.5 %copy-start.1 = (f32[1,512,512]{2,1,0:T(8,128)S(1)}, f32[1,512,512]{2,1,0:T(8,128)}, u32[]{:S(2)}) copy-start(f32[1,512,512]{2,1,0:T(8,128)} %param.7) | copy-start | bytes 3145732
  24.2 25.5 %copy-start.2 = (f32[1,512,512]{2,1,0:T(8,128)S(1)}, f32[1,512,512]{2,1,0:T(8,128)}, u32[]{:S(2)}) copy-start(f32[1,512,512]{2,1,0:T(8,128)} %param.5) | copy-start | bytes 3145732
  24.9 37.8 %collective-permute-start.4 = (f32[512,256]{1,0:T(8,128)S(1)}, f32[512,256]{1,0:T(8,128)S(1)}, u32[]{:S(2)}, u32[]{:S(2)}) collective-permute-start(f32[512,256]{1,0:T(8,128)S(1)} %get-tuple-element.30), channel_id=1, source_target_pairs={{0,1},{1,2},{2,3},{3,4},{4,5},{5,6},{6,7},{7,8},{8,9},{9,10},{10,1... | collective-permute-start | bytes 1572872 | tf_op jit(solution)/shard_map/ppermute | solution.py:21
  27.0 35.8 %copy-start.7 = (f32[1,512,128]{2,1,0:T(8,128)S(1)}, f32[1,512,128]{2,1,0:T(8,128)}, u32[]{:S(2)}) copy-start(f32[1,512,128]{2,1,0:T(8,128)} %param.8) | copy-start | bytes 786436
  27.0 35.7 %collective-permute-start.5 = (f32[512,256]{1,0:T(8,128)S(1)}, f32[512,256]{1,0:T(8,128)S(1)}, u32[]{:S(2)}, u32[]{:S(2)}) collective-permute-start(f32[512,256]{1,0:T(8,128)S(1)} %get-tuple-element.31), channel_id=1, source_target_pairs={{1,0},{2,1},{3,2},{4,3},{5,4},{6,5},{7,6},{8,7},{9,8},{10,9},{11,1... | collective-permute-start | bytes 1572872 | tf_op jit(solution)/shard_map/ppermute | solution.py:21
  55.3 44.7 %collective-permute-start.6 = (f32[512,512]{1,0:T(8,128)S(1)}, f32[512,512]{1,0:T(8,128)S(1)}, u32[]{:S(2)}, u32[]{:S(2)}) collective-permute-start(f32[512,512]{1,0:T(8,128)S(1)} %get-tuple-element.35), channel_id=1, source_target_pairs={{0,1},{1,2},{2,3},{3,4},{4,5},{5,6},{6,7},{7,8},{8,9},{9,10},{10,1... | collective-permute-start | bytes 3145736 | tf_op jit(solution)/shard_map/ppermute | solution.py:21
  57.2 45.7 %collective-permute-start.10 = (f32[512,512]{1,0:T(8,128)S(1)}, f32[512,512]{1,0:T(8,128)S(1)}, u32[]{:S(2)}, u32[]{:S(2)}) collective-permute-start(f32[512,512]{1,0:T(8,128)S(1)} %get-tuple-element.38), channel_id=1, source_target_pairs={{1,0},{2,1},{3,2},{4,3},{5,4},{6,5},{7,6},{8,7},{9,8},{10,9},{11,1... | collective-permute-start | bytes 3145736 | tf_op jit(solution)/shard_map/ppermute | solution.py:21
  62.7 37.2 %copy-start.6 = (f32[512,512]{1,0:T(8,128)S(1)}, f32[512,512]{1,0:T(8,128)}, u32[]{:S(2)}) copy-start(f32[512,512]{1,0:T(8,128)} %get-tuple-element.34.scaled_low.left.left_a) | copy-start | bytes 3145732
  64.4 44.5 %collective-permute-start.8 = (f32[512,128]{1,0:T(8,128)S(1)}, f32[512,128]{1,0:T(8,128)S(1)}, u32[]{:S(2)}, u32[]{:S(2)}) collective-permute-start(f32[512,128]{1,0:T(8,128)S(1)} %get-tuple-element.32), channel_id=1, source_target_pairs={{0,1},{1,2},{2,3},{3,4},{4,5},{5,6},{6,7},{7,8},{8,9},{9,10},{10,1... | collective-permute-start | bytes 786440 | tf_op jit(solution)/shard_map/ppermute | solution.py:21
  66.3 36.6 %copy-start.4 = (f32[512,512]{1,0:T(8,128)S(1)}, f32[512,512]{1,0:T(8,128)}, u32[]{:S(2)}) copy-start(f32[512,512]{1,0:T(8,128)} %get-tuple-element.37.scaled_up.left.left_b) | copy-start | bytes 3145732
  66.3 42.6 %collective-permute-start.9 = (f32[512,128]{1,0:T(8,128)S(1)}, f32[512,128]{1,0:T(8,128)S(1)}, u32[]{:S(2)}, u32[]{:S(2)}) collective-permute-start(f32[512,128]{1,0:T(8,128)S(1)} %get-tuple-element.33), channel_id=1, source_target_pairs={{1,0},{2,1},{3,2},{4,3},{5,4},{6,5},{7,6},{8,7},{9,8},{10,9},{11,1... | collective-permute-start | bytes 786440 | tf_op jit(solution)/shard_map/ppermute | solution.py:21
  100.9 24.8 %collective-permute-start.7 = (f32[512,512]{1,0:T(8,128)S(1)}, f32[512,512]{1,0:T(8,128)S(1)}, u32[]{:S(2)}, u32[]{:S(2)}) collective-permute-start(f32[512,512]{1,0:T(8,128)S(1)} %shard_map.59), channel_id=1, source_target_pairs={{0,1},{1,2},{2,3},{3,4},{4,5},{5,6},{6,7},{7,8},{8,9},{9,10},{10,1... | collective-permute-start | bytes 3145736 | tf_op jit(solution)/shard_map/ppermute | solution.py:21
  103.9 23.7 %collective-permute-start.13 = (f32[512,512]{1,0:T(8,128)S(1)}, f32[512,512]{1,0:T(8,128)S(1)}, u32[]{:S(2)}, u32[]{:S(2)}) collective-permute-start(f32[512,512]{1,0:T(8,128)S(1)} %shard_map.61), channel_id=1, source_target_pairs={{1,0},{2,1},{3,2},{4,3},{5,4},{6,5},{7,6},{8,7},{9,8},{10,9},{11,1... | collective-permute-start | bytes 3145736 | tf_op jit(solution)/shard_map/ppermute | solution.py:21
  109.7 11.4 %collective-permute-start.11 = (f32[512,128]{1,0:T(8,128)S(1)}, f32[512,128]{1,0:T(8,128)S(1)}, u32[]{:S(2)}, u32[]{:S(2)}) collective-permute-start(f32[512,128]{1,0:T(8,128)S(1)} %get-tuple-element.41), channel_id=1, source_target_pairs={{0,1},{1,2},{2,3},{3,4},{4,5},{5,6},{6,7},{7,8},{8,9},{9,10},{10,1... | collective-permute-start | bytes 786440 | tf_op jit(solution)/shard_map/ppermute | solution.py:21
  111.6 13.4 %collective-permute-start.12 = (f32[512,128]{1,0:T(8,128)S(1)}, f32[512,128]{1,0:T(8,128)S(1)}, u32[]{:S(2)}, u32[]{:S(2)}) collective-permute-start(f32[512,128]{1,0:T(8,128)S(1)} %get-tuple-element.42), channel_id=1, source_target_pairs={{1,0},{2,1},{3,2},{4,3},{5,4},{6,5},{7,6},{8,7},{9,8},{10,9},{11,1... | collective-permute-start | bytes 786440 | tf_op jit(solution)/shard_map/ppermute | solution.py:21

commit v2 on v1

--- a/solution.py
+++ b/solution.py
@@ -117,10 +117,6 @@
     out_b[...] = multiply(split(left_b[...]), split(right_b[...]))
 
 
-def inner_kernel(rhs1, low, up, d_l, d_r, out):
-    out[...] = rhs1[...] + multiply(split(low[...]), split(d_l[...])) + multiply(split(up[...]), split(d_r[...]))
-
-
 def triple(first, second, third):
     return multiply(split(multiply(split(first), split(second))), split(third))
 
@@ -129,12 +125,17 @@
     out[...] = base[...] - triple(first[...], second[...], third[...])
 
 
-def last_kernel(base, first, second, third, inner_ref, out):
-    rest, scale = residual(base[...] - triple(first[...], second[...], third[...]))
-    halves = split(rest)
-    inner = inner_ref[...]
+def last_kernel(base, first, second, third, rest, scale):
+    value, factor = residual(base[...] - triple(first[...], second[...], third[...]))
+    rest[...] = value
+    scale[...] = jnp.broadcast_to(factor, scale.shape)
+
+
+def final_kernel(rest, scale, rhs1, low, up, d_l, d_r, out):
+    inner = rhs1[...] + multiply(split(low[...]), split(d_l[...])) + multiply(split(up[...]), split(d_r[...]))
+    halves = split(rest[...])
     part = inner + multiply(halves, split(multiply(halves, split(inner))))
-    out[...] = (part + multiply(halves, split(part))) * scale
+    out[...] = (part + multiply(halves, split(part))) * scale[0:1, 0:1]
 
 
 def call(kernel, outs, *args, weight=0, limit=VMEM_LIMIT, **options):
@@ -173,8 +174,8 @@
     vec_l = shifted(to_up, 1)
     vec_r = shifted(to_down, -1)
     diag1, pivot1, next_up, next_down = call(second_kernel, (square,) * 4, diag, low, up, up_l, low_r)
+    next_r = shifted(next_down, -1)
     next_l = shifted(next_up, 1)
-    next_r = shifted(next_down, -1)
     rhs1, w_up, w_down = call(
         middle_kernel, (tall,) * 3, low, up, rhs, pivot1, vec_l, vec_r, weight=MIDDLE_WEIGHT
     )
@@ -189,10 +190,10 @@
     d_up, d_down = call(two_pairs_kernel, (tall, tall), scaled_low, w_l, scaled_up, w_r, weight=PASS_WEIGHT)
     d_l = shifted(d_up, 1)
     d_r = shifted(d_down, -1)
-    (inner,) = call(inner_kernel, (tall,), rhs1, low, up, d_l, d_r)
     (part2,) = call(before_last_kernel, (square,), diag1, low, pass_l, up_l)
-    part2, inner = lax.optimization_barrier((part2, inner))
-    (out,) = call(last_kernel, (tall,), part2, up, pass_r, low_r, inner)
+    rest, scale = call(last_kernel, (square, (8, 128)), part2, up, pass_r, low_r)
+    d_l, d_r, rest = lax.optimization_barrier((d_l, d_r, rest))
+    (out,) = call(final_kernel, (tall,), rest, scale, rhs1, low, up, d_l, d_r)
     return out[None]
 
 

time: 132 us -> 131 us (level)
  the two profiles are of different devices: /device:TPU:161 before, /device:TPU:126 now
where the time goes in v2:
time: 131 us; the launch traced here: 130 us
  waiting for transfers between devices  55 us (42%)
  starting transfers between devices  47.4 us (36%)
  Pallas kernels  23.9 us (18%)
  local copies, waits for them, and re-layouts  3.44 us (3%)
    ppermute x14, waiting for transfers between devices, shifted(): lax.ppermute(value, AXES, [(source, source + steps) for source in range(i...  55 us
    ppermute x14, starting transfers between devices, shifted(): lax.ppermute(value, AXES, [(source, source + steps) for source in range(i...  47.4 us
    pallas_call x10, Pallas kernels, call(): pl.pallas_call(kernel, out_shape=[jax.ShapeDtypeStruct(shape, jnp.float32...  23.9 us
    unnamed x18, local copies, waits for them, and re-layouts  3.44 us
  transfers between devices with their start and end apart: 14, of which 7 were waited for; matrix products, arithmetic and copies ran while one was open for 0% of the time, Pallas kernels for 16%

profile of v2, /device:TPU:126, one launch (start us, length us, event | category | flops | bytes accessed | tf_op | source)
XLA Modules:
  0.0 130.0 jit_solution(3548712851650944056)
XLA Ops:
  0.0 2.6 %collective-permute-start.3 = (f32[512,128]{1,0:T(8,128)}, f32[512,128]{1,0:T(8,128)S(1)}, u32[]{:S(2)}, u32[]{:S(2)}) collective-permute-start(f32[512,128]{1,0:T(8,128)} %bitcast.20), channel_id=1, source_target_pairs={{1,0},{2,1},{3,2},{4,3},{5,4},{6,5},{7,6},{8,7},{9,8},{10,9},{11,1... | collective-permute-start | bytes 786440 | tf_op jit(solution)/shard_map/ppermute | solution.py:21
  2.6 4.1 %collective-permute-start.2 = (f32[512,128]{1,0:T(8,128)}, f32[512,128]{1,0:T(8,128)S(1)}, u32[]{:S(2)}, u32[]{:S(2)}) collective-permute-start(f32[512,128]{1,0:T(8,128)} %bitcast.21), channel_id=1, source_target_pairs={{0,1},{1,2},{2,3},{3,4},{4,5},{5,6},{6,7},{7,8},{8,9},{9,10},{10,1... | collective-permute-start | bytes 786440 | tf_op jit(solution)/shard_map/ppermute | solution.py:21
  6.8 6.8 %shard_map.55 = (f32[512,512]{1,0:T(8,128)}, f32[512,512]{1,0:T(8,128)}, f32[512,128]{1,0:T(8,128)}) custom-call(f32[512,512]{1,0:T(8,128)} %bitcast.16, f32[512,512]{1,0:T(8,128)} %bitcast.6, f32[512,512]{1,0:T(8,128)} %bitcast.11, f32[512,128]{1,0:T(8,128)} %bitcast.18), custom_call_target="tpu_custom_call" | custom-call | tf_op jit(solution)/shard_map/pallas_call | solution.py:144
  13.6 1.9 %collective-permute-start.1 = (f32[512,512]{1,0:T(8,128)}, f32[512,512]{1,0:T(8,128)S(1)}, u32[]{:S(2)}, u32[]{:S(2)}) collective-permute-start(f32[512,512]{1,0:T(8,128)} %get-tuple-element.36.scaled_low.left.left_a), channel_id=1, source_target_pairs={{1,0},{2,1},{3,2},{4,3},{5,4},{6,5},{7,6},{8,7},{9,8},{10,9},{11,1... | collective-permute-start | bytes 3145736 | tf_op jit(solution)/shard_map/ppermute | solution.py:21
  15.5 4.9 %collective-permute-start = (f32[512,512]{1,0:T(8,128)}, f32[512,512]{1,0:T(8,128)S(1)}, u32[]{:S(2)}, u32[]{:S(2)}) collective-permute-start(f32[512,512]{1,0:T(8,128)} %get-tuple-element.38.scaled_up.left.left_b), channel_id=1, source_target_pairs={{0,1},{1,2},{2,3},{3,4},{4,5},{5,6},{6,7},{7,8},{8,9},{9,10},{10,1... | collective-permute-start | bytes 3145736 | tf_op jit(solution)/shard_map/ppermute | solution.py:21
  20.4 0.0 collective-permute-done.3.guess_r
  20.4 0.0 collective-permute-done.2.guess_l
  20.4 0.0 copy-start.3
  20.4 1.2 copy-done.3
  21.7 0.0 copy-start.5
  21.7 1.2 copy-done.5
  22.9 0.0 copy-start.8
  22.9 0.9 copy-done.8
  23.9 0.0 copy-start
  23.9 0.0 copy-start.1
  23.9 0.0 copy-start.2
  23.9 0.7 shard_map.57
  24.6 2.1 %collective-permute-start.4 = (f32[512,256]{1,0:T(8,128)S(1)}, f32[512,256]{1,0:T(8,128)S(1)}, u32[]{:S(2)}, u32[]{:S(2)}) collective-permute-start(f32[512,256]{1,0:T(8,128)S(1)} %get-tuple-element.32), channel_id=1, source_target_pairs={{0,1},{1,2},{2,3},{3,4},{4,5},{5,6},{6,7},{7,8},{8,9},{9,10},{10,1... | collective-permute-start | bytes 1572872 | tf_op jit(solution)/shard_map/ppermute | solution.py:21
  26.7 0.0 copy-start.7
  26.7 4.0 %collective-permute-start.5 = (f32[512,256]{1,0:T(8,128)S(1)}, f32[512,256]{1,0:T(8,128)S(1)}, u32[]{:S(2)}, u32[]{:S(2)}) collective-permute-start(f32[512,256]{1,0:T(8,128)S(1)} %get-tuple-element.33), channel_id=1, source_target_pairs={{1,0},{2,1},{3,2},{4,3},{5,4},{6,5},{7,6},{8,7},{9,8},{10,9},{11,1... | collective-permute-start | bytes 1572872 | tf_op jit(solution)/shard_map/ppermute | solution.py:21
  30.7 11.7 %collective-permute-done.1.low_r.third = f32[512,512]{1,0:T(8,128)S(1)} collective-permute-done((f32[512,512]{1,0:T(8,128)}, f32[512,512]{1,0:T(8,128)S(1)}, u32[]{:S(2)}, u32[]{:S(2)}) %collective-permute-start.1) | collective-permute-done | bytes 1048608 | tf_op jit(solution)/shard_map/ppermute | solution.py:21
  42.4 7.5 %collective-permute-done.up_l.third = f32[512,512]{1,0:T(8,128)S(1)} collective-permute-done((f32[512,512]{1,0:T(8,128)}, f32[512,512]{1,0:T(8,128)S(1)}, u32[]{:S(2)}, u32[]{:S(2)}) %collective-permute-start) | collective-permute-done | bytes 1048608 | tf_op jit(solution)/shard_map/ppermute | solution.py:21
  49.9 0.0 copy-done
  49.9 0.0 copy-done.1
  49.9 0.0 copy-done.2
  49.9 5.6 %shard_map.56 = (f32[512,512]{1,0:T(8,128)S(1)}, f32[512,512]{1,0:T(8,128)S(1)}, f32[512,512]{1,0:T(8,128)S(1)}, f32[512,512]{1,0:T(8,128)S(1)}) custom-call(f32[512,512]{1,0:T(8,128)S(1)} %bitcast.17, f32[512,512]{1,0:T(8,128)S(1)} %bitcast.7, f32[512,512]{1,0:T(8,128)S(1)} %bitcast.12, f32[512,512]{1,0:T(8,128)S(1)} %collective-permute-done.up_l.third, ...), custom_call_target="tpu_custom_call" | custom-call | tf_op jit(solution)/shard_map/pallas_call | solution.py:144
  55.5 4.9 %collective-permute-start.8 = (f32[512,512]{1,0:T(8,128)S(1)}, f32[512,512]{1,0:T(8,128)S(1)}, u32[]{:S(2)}, u32[]{:S(2)}) collective-permute-start(f32[512,512]{1,0:T(8,128)S(1)} %get-tuple-element.37), channel_id=1, source_target_pairs={{0,1},{1,2},{2,3},{3,4},{4,5},{5,6},{6,7},{7,8},{8,9},{9,10},{10,1... | collective-permute-start | bytes 3145736 | tf_op jit(solution)/shard_map/ppermute | solution.py:21
  60.4 1.9 %collective-permute-start.9 = (f32[512,512]{1,0:T(8,128)S(1)}, f32[512,512]{1,0:T(8,128)S(1)}, u32[]{:S(2)}, u32[]{:S(2)}) collective-permute-start(f32[512,512]{1,0:T(8,128)S(1)} %get-tuple-element.39), channel_id=1, source_target_pairs={{1,0},{2,1},{3,2},{4,3},{5,4},{6,5},{7,6},{8,7},{9,8},{10,9},{11,1... | collective-permute-start | bytes 3145736 | tf_op jit(solution)/shard_map/ppermute | solution.py:21
  62.4 7.1 %collective-permute-done.4.vec_l = f32[512,256]{1,0:T(8,128)S(1)} collective-permute-done((f32[512,256]{1,0:T(8,128)S(1)}, f32[512,256]{1,0:T(8,128)S(1)}, u32[]{:S(2)}, u32[]{:S(2)}) %collective-permute-start.4) | collective-permute-done | bytes 524320 | tf_op jit(solution)/shard_map/ppermute | solution.py:21
  69.5 0.0 collective-permute-done.5.vec_r
  69.5 0.0 copy-done.7
  69.5 0.0 copy-start.6
  69.5 1.6 %shard_map.58 = (f32[512,128]{1,0:T(8,128)S(1)}, f32[512,128]{1,0:T(8,128)S(1)}, f32[512,128]{1,0:T(8,128)S(1)}) custom-call(f32[512,512]{1,0:T(8,128)S(1)} %bitcast.8, f32[512,512]{1,0:T(8,128)S(1)} %bitcast.13, f32[512,128]{1,0:T(8,128)S(1)} %bitcast.19, f32[512,512]{1,0:T(8,128)S(1)} %get-tuple-element.30.pivot1, ...), custom_call_target="tpu_custom_call" | custom-call | flops 10000000000 | tf_op jit(solution)/shard_map/pallas_call | solution.py:144
  71.1 5.0 %collective-permute-start.6 = (f32[512,128]{1,0:T(8,128)S(1)}, f32[512,128]{1,0:T(8,128)S(1)}, u32[]{:S(2)}, u32[]{:S(2)}) collective-permute-start(f32[512,128]{1,0:T(8,128)S(1)} %get-tuple-element.34), channel_id=1, source_target_pairs={{0,1},{1,2},{2,3},{3,4},{4,5},{5,6},{6,7},{7,8},{8,9},{9,10},{10,1... | collective-permute-start | bytes 786440 | tf_op jit(solution)/shard_map/ppermute | solution.py:21
  76.1 0.0 copy-start.4
  76.1 2.1 %collective-permute-start.7 = (f32[512,128]{1,0:T(8,128)S(1)}, f32[512,128]{1,0:T(8,128)S(1)}, u32[]{:S(2)}, u32[]{:S(2)}) collective-permute-start(f32[512,128]{1,0:T(8,128)S(1)} %get-tuple-element.35), channel_id=1, source_target_pairs={{1,0},{2,1},{3,2},{4,3},{5,4},{6,5},{7,6},{8,7},{9,8},{10,9},{11,1... | collective-permute-start | bytes 786440 | tf_op jit(solution)/shard_map/ppermute | solution.py:21
  78.2 16.5 %collective-permute-done.8.right = f32[512,512]{1,0:T(8,128)S(1)} collective-permute-done((f32[512,512]{1,0:T(8,128)S(1)}, f32[512,512]{1,0:T(8,128)S(1)}, u32[]{:S(2)}, u32[]{:S(2)}) %collective-permute-start.8) | collective-permute-done | bytes 1048608 | tf_op jit(solution)/shard_map/ppermute | solution.py:21
  94.7 0.0 copy-done.6
  94.7 1.0 shard_map.59
  95.7 5.0 %collective-permute-start.12 = (f32[512,512]{1,0:T(8,128)S(1)}, f32[512,512]{1,0:T(8,128)S(1)}, u32[]{:S(2)}, u32[]{:S(2)}) collective-permute-start(f32[512,512]{1,0:T(8,128)S(1)} %shard_map.59), channel_id=1, source_target_pairs={{0,1},{1,2},{2,3},{3,4},{4,5},{5,6},{6,7},{7,8},{8,9},{9,10},{10,1... | collective-permute-start | bytes 3145736 | tf_op jit(solution)/shard_map/ppermute | solution.py:21
  100.7 0.0 collective-permute-done.9.right
  100.7 0.0 copy-done.4
  100.8 1.0 shard_map.60
  101.7 2.1 %collective-permute-start.13 = (f32[512,512]{1,0:T(8,128)S(1)}, f32[512,512]{1,0:T(8,128)S(1)}, u32[]{:S(2)}, u32[]{:S(2)}) collective-permute-start(f32[512,512]{1,0:T(8,128)S(1)} %shard_map.60), channel_id=1, source_target_pairs={{1,0},{2,1},{3,2},{4,3},{5,4},{6,5},{7,6},{8,7},{9,8},{10,9},{11,1... | collective-permute-start | bytes 3145736 | tf_op jit(solution)/shard_map/ppermute | solution.py:21
  103.9 0.0 collective-permute-done.6.right_a
  103.9 0.0 collective-permute-done.7.right_b
  103.9 0.7 shard_map.61
  104.6 4.9 %collective-permute-start.10 = (f32[512,128]{1,0:T(8,128)S(1)}, f32[512,128]{1,0:T(8,128)S(1)}, u32[]{:S(2)}, u32[]{:S(2)}) collective-permute-start(f32[512,128]{1,0:T(8,128)S(1)} %get-tuple-element.42), channel_id=1, source_target_pairs={{0,1},{1,2},{2,3},{3,4},{4,5},{5,6},{6,7},{7,8},{8,9},{9,10},{10,1... | collective-permute-start | bytes 786440 | tf_op jit(solution)/shard_map/ppermute | solution.py:21
  109.5 1.9 %collective-permute-start.11 = (f32[512,128]{1,0:T(8,128)S(1)}, f32[512,128]{1,0:T(8,128)S(1)}, u32[]{:S(2)}, u32[]{:S(2)}) collective-permute-start(f32[512,128]{1,0:T(8,128)S(1)} %get-tuple-element.43), channel_id=1, source_target_pairs={{1,0},{2,1},{3,2},{4,3},{5,4},{6,5},{7,6},{8,7},{9,8},{10,9},{11,1... | collective-permute-start | bytes 786440 | tf_op jit(solution)/shard_map/ppermute | solution.py:21
  111.4 1.6 %collective-permute-done.12.second = f32[512,512]{1,0:T(8,128)S(1)} collective-permute-done((f32[512,512]{1,0:T(8,128)S(1)}, f32[512,512]{1,0:T(8,128)S(1)}, u32[]{:S(2)}, u32[]{:S(2)}) %collective-permute-start.12) | collective-permute-done | bytes 1048608 | tf_op jit(solution)/shard_map/ppermute | solution.py:21
  113.0 1.8 %shard_map.62.base = f32[512,512]{1,0:T(8,128)S(1)} custom-call(f32[512,512]{1,0:T(8,128)S(1)} %get-tuple-element.44.base, f32[512,512]{1,0:T(8,128)S(1)} %bitcast.9, f32[512,512]{1,0:T(8,128)S(1)} %collective-permute-done.12.second, f32[512,512]{1,0:T(8,128)S(1)} %collective-permute-done.up_l.third), custom_call_target="tpu_custom_call" | custom-call | tf_op jit(solution)/shard_map/pallas_call | solution.py:144
  114.8 9.9 %collective-permute-done.13.second = f32[512,512]{1,0:T(8,128)S(1)} collective-permute-done((f32[512,512]{1,0:T(8,128)S(1)}, f32[512,512]{1,0:T(8,128)S(1)}, u32[]{:S(2)}, u32[]{:S(2)}) %collective-permute-start.13) | collective-permute-done | bytes 1048608 | tf_op jit(solution)/shard_map/ppermute | solution.py:21
  124.7 2.1 %shard_map.63 = (f32[512,512]{1,0:T(8,128)S(1)}, f32[8,128]{1,0:T(8,128)S(1)}) custom-call(f32[512,512]{1,0:T(8,128)S(1)} %shard_map.62.base, f32[512,512]{1,0:T(8,128)S(1)} %bitcast.14, f32[512,512]{1,0:T(8,128)S(1)} %collective-permute-done.13.second, f32[512,512]{1,0:T(8,128)S(1)} %collective-permute-done.1.low_r.third), custom_call_target="tpu_custom_call" | custom-call | tf_op jit(solution)/shard_map/pallas_call | solution.py:144
  126.8 0.0 collective-permute-done.10.d_l
  126.9 0.7 collective-permute-done.11.d_r
  127.6 2.5 %shard_map.64 = f32[512,128]{1,0:T(8,128)} custom-call(f32[512,512]{1,0:T(8,128)S(1)} %get-tuple-element.46.rest, f32[8,128]{1,0:T(8,128)S(1)} %get-tuple-element.47.scale, f32[512,128]{1,0:T(8,128)S(1)} %get-tuple-element.48.rhs1, f32[512,512]{1,0:T(8,128)S(1)} %bitcast.10, f32[512,512]{1,0:T(8,128)S(1)} %bitcast.15, ...), custom_call_target="tpu_custom_call" | custom-call | tf_op jit(solution)/shard_map/pallas_call | solution.py:144
Async XLA Ops:
  0.0 20.4 %collective-permute-start.3 = (f32[512,128]{1,0:T(8,128)}, f32[512,128]{1,0:T(8,128)S(1)}, u32[]{:S(2)}, u32[]{:S(2)}) collective-permute-start(f32[512,128]{1,0:T(8,128)} %bitcast.20), channel_id=1, source_target_pairs={{1,0},{2,1},{3,2},{4,3},{5,4},{6,5},{7,6},{8,7},{9,8},{10,9},{11,1... | collective-permute-start | bytes 786440 | tf_op jit(solution)/shard_map/ppermute | solution.py:21
  2.6 17.8 %collective-permute-start.2 = (f32[512,128]{1,0:T(8,128)}, f32[512,128]{1,0:T(8,128)S(1)}, u32[]{:S(2)}, u32[]{:S(2)}) collective-permute-start(f32[512,128]{1,0:T(8,128)} %bitcast.21), channel_id=1, source_target_pairs={{0,1},{1,2},{2,3},{3,4},{4,5},{5,6},{6,7},{7,8},{8,9},{9,10},{10,1... | collective-permute-start | bytes 786440 | tf_op jit(solution)/shard_map/ppermute | solution.py:21
  13.6 28.8 %collective-permute-start.1 = (f32[512,512]{1,0:T(8,128)}, f32[512,512]{1,0:T(8,128)S(1)}, u32[]{:S(2)}, u32[]{:S(2)}) collective-permute-start(f32[512,512]{1,0:T(8,128)} %get-tuple-element.36.scaled_low.left.left_a), channel_id=1, source_target_pairs={{1,0},{2,1},{3,2},{4,3},{5,4},{6,5},{7,6},{8,7},{9,8},{10,9},{11,1... | collective-permute-start | bytes 3145736 | tf_op jit(solution)/shard_map/ppermute | solution.py:21
  15.5 34.3 %collective-permute-start = (f32[512,512]{1,0:T(8,128)}, f32[512,512]{1,0:T(8,128)S(1)}, u32[]{:S(2)}, u32[]{:S(2)}) collective-permute-start(f32[512,512]{1,0:T(8,128)} %get-tuple-element.38.scaled_up.left.left_b), channel_id=1, source_target_pairs={{0,1},{1,2},{2,3},{3,4},{4,5},{5,6},{6,7},{7,8},{8,9},{9,10},{10,1... | collective-permute-start | bytes 3145736 | tf_op jit(solution)/shard_map/ppermute | solution.py:21
  20.4 1.3 copy-start.3
  21.7 1.2 copy-start.5
  22.9 0.9 copy-start.8
  23.9 26.0 %copy-start = (f32[1,512,512]{2,1,0:T(8,128)S(1)}, f32[1,512,512]{2,1,0:T(8,128)}, u32[]{:S(2)}) copy-start(f32[1,512,512]{2,1,0:T(8,128)} %param.6) | copy-start | bytes 3145732
  23.9 26.0 %copy-start.1 = (f32[1,512,512]{2,1,0:T(8,128)S(1)}, f32[1,512,512]{2,1,0:T(8,128)}, u32[]{:S(2)}) copy-start(f32[1,512,512]{2,1,0:T(8,128)} %param.7) | copy-start | bytes 3145732
  23.9 26.0 %copy-start.2 = (f32[1,512,512]{2,1,0:T(8,128)S(1)}, f32[1,512,512]{2,1,0:T(8,128)}, u32[]{:S(2)}) copy-start(f32[1,512,512]{2,1,0:T(8,128)} %param.5) | copy-start | bytes 3145732
  24.6 44.9 %collective-permute-start.4 = (f32[512,256]{1,0:T(8,128)S(1)}, f32[512,256]{1,0:T(8,128)S(1)}, u32[]{:S(2)}, u32[]{:S(2)}) collective-permute-start(f32[512,256]{1,0:T(8,128)S(1)} %get-tuple-element.32), channel_id=1, source_target_pairs={{0,1},{1,2},{2,3},{3,4},{4,5},{5,6},{6,7},{7,8},{8,9},{9,10},{10,1... | collective-permute-start | bytes 1572872 | tf_op jit(solution)/shard_map/ppermute | solution.py:21
  26.7 42.8 %copy-start.7 = (f32[1,512,128]{2,1,0:T(8,128)S(1)}, f32[1,512,128]{2,1,0:T(8,128)}, u32[]{:S(2)}) copy-start(f32[1,512,128]{2,1,0:T(8,128)} %param.8) | copy-start | bytes 786436
  26.7 42.8 %collective-permute-start.5 = (f32[512,256]{1,0:T(8,128)S(1)}, f32[512,256]{1,0:T(8,128)S(1)}, u32[]{:S(2)}, u32[]{:S(2)}) collective-permute-start(f32[512,256]{1,0:T(8,128)S(1)} %get-tuple-element.33), channel_id=1, source_target_pairs={{1,0},{2,1},{3,2},{4,3},{5,4},{6,5},{7,6},{8,7},{9,8},{10,9},{11,1... | collective-permute-start | bytes 1572872 | tf_op jit(solution)/shard_map/ppermute | solution.py:21
  55.5 39.2 %collective-permute-start.8 = (f32[512,512]{1,0:T(8,128)S(1)}, f32[512,512]{1,0:T(8,128)S(1)}, u32[]{:S(2)}, u32[]{:S(2)}) collective-permute-start(f32[512,512]{1,0:T(8,128)S(1)} %get-tuple-element.37), channel_id=1, source_target_pairs={{0,1},{1,2},{2,3},{3,4},{4,5},{5,6},{6,7},{7,8},{8,9},{9,10},{10,1... | collective-permute-start | bytes 3145736 | tf_op jit(solution)/shard_map/ppermute | solution.py:21
  60.4 40.3 %collective-permute-start.9 = (f32[512,512]{1,0:T(8,128)S(1)}, f32[512,512]{1,0:T(8,128)S(1)}, u32[]{:S(2)}, u32[]{:S(2)}) collective-permute-start(f32[512,512]{1,0:T(8,128)S(1)} %get-tuple-element.39), channel_id=1, source_target_pairs={{1,0},{2,1},{3,2},{4,3},{5,4},{6,5},{7,6},{8,7},{9,8},{10,9},{11,1... | collective-permute-start | bytes 3145736 | tf_op jit(solution)/shard_map/ppermute | solution.py:21
  69.5 25.2 %copy-start.6 = (f32[512,512]{1,0:T(8,128)S(1)}, f32[512,512]{1,0:T(8,128)}, u32[]{:S(2)}) copy-start(f32[512,512]{1,0:T(8,128)} %get-tuple-element.36.scaled_low.left.left_a) | copy-start | bytes 3145732
  71.1 32.8 %collective-permute-start.6 = (f32[512,128]{1,0:T(8,128)S(1)}, f32[512,128]{1,0:T(8,128)S(1)}, u32[]{:S(2)}, u32[]{:S(2)}) collective-permute-start(f32[512,128]{1,0:T(8,128)S(1)} %get-tuple-element.34), channel_id=1, source_target_pairs={{0,1},{1,2},{2,3},{3,4},{4,5},{5,6},{6,7},{7,8},{8,9},{9,10},{10,1... | collective-permute-start | bytes 786440 | tf_op jit(solution)/shard_map/ppermute | solution.py:21
  76.1 24.6 %copy-start.4 = (f32[512,512]{1,0:T(8,128)S(1)}, f32[512,512]{1,0:T(8,128)}, u32[]{:S(2)}) copy-start(f32[512,512]{1,0:T(8,128)} %get-tuple-element.38.scaled_up.left.left_b) | copy-start | bytes 3145732
  76.1 27.8 %collective-permute-start.7 = (f32[512,128]{1,0:T(8,128)S(1)}, f32[512,128]{1,0:T(8,128)S(1)}, u32[]{:S(2)}, u32[]{:S(2)}) collective-permute-start(f32[512,128]{1,0:T(8,128)S(1)} %get-tuple-element.35), channel_id=1, source_target_pairs={{1,0},{2,1},{3,2},{4,3},{5,4},{6,5},{7,6},{8,7},{9,8},{10,9},{11,1... | collective-permute-start | bytes 786440 | tf_op jit(solution)/shard_map/ppermute | solution.py:21
  95.7 17.3 %collective-permute-start.12 = (f32[512,512]{1,0:T(8,128)S(1)}, f32[512,512]{1,0:T(8,128)S(1)}, u32[]{:S(2)}, u32[]{:S(2)}) collective-permute-start(f32[512,512]{1,0:T(8,128)S(1)} %shard_map.59), channel_id=1, source_target_pairs={{0,1},{1,2},{2,3},{3,4},{4,5},{5,6},{6,7},{7,8},{8,9},{9,10},{10,1... | collective-permute-start | bytes 3145736 | tf_op jit(solution)/shard_map/ppermute | solution.py:21
  101.7 23.0 %collective-permute-start.13 = (f32[512,512]{1,0:T(8,128)S(1)}, f32[512,512]{1,0:T(8,128)S(1)}, u32[]{:S(2)}, u32[]{:S(2)}) collective-permute-start(f32[512,512]{1,0:T(8,128)S(1)} %shard_map.60), channel_id=1, source_target_pairs={{1,0},{2,1},{3,2},{4,3},{5,4},{6,5},{7,6},{8,7},{9,8},{10,9},{11,1... | collective-permute-start | bytes 3145736 | tf_op jit(solution)/shard_map/ppermute | solution.py:21
  104.6 22.3 %collective-permute-start.10 = (f32[512,128]{1,0:T(8,128)S(1)}, f32[512,128]{1,0:T(8,128)S(1)}, u32[]{:S(2)}, u32[]{:S(2)}) collective-permute-start(f32[512,128]{1,0:T(8,128)S(1)} %get-tuple-element.42), channel_id=1, source_target_pairs={{0,1},{1,2},{2,3},{3,4},{4,5},{5,6},{6,7},{7,8},{8,9},{9,10},{10,1... | collective-permute-start | bytes 786440 | tf_op jit(solution)/shard_map/ppermute | solution.py:21
  109.5 18.1 %collective-permute-start.11 = (f32[512,128]{1,0:T(8,128)S(1)}, f32[512,128]{1,0:T(8,128)S(1)}, u32[]{:S(2)}, u32[]{:S(2)}) collective-permute-start(f32[512,128]{1,0:T(8,128)S(1)} %get-tuple-element.43), channel_id=1, source_target_pairs={{1,0},{2,1},{3,2},{4,3},{5,4},{6,5},{7,6},{8,7},{9,8},{10,9},{11,1... | collective-permute-start | bytes 786440 | tf_op jit(solution)/shard_map/ppermute | solution.py:21

commit v3 on v2

--- a/solution.py
+++ b/solution.py
@@ -171,6 +171,7 @@
     to_up, to_down = call(
         vector_kernel, (wide, wide), scaled_up, scaled_low, scaled_rhs, guess_l, guess_r, weight=VECTOR_WEIGHT
     )
+    low_r, to_up, to_down = lax.optimization_barrier((low_r, to_up, to_down))
     vec_l = shifted(to_up, 1)
     vec_r = shifted(to_down, -1)
     diag1, pivot1, next_up, next_down = call(second_kernel, (square,) * 4, diag, low, up, up_l, low_r)

time: 131 us -> 127 us (0.969)
  starting transfers between devices: 47.4 us -> 45.4 us
    ppermute x14, starting transfers between devices: 47.4 us -> 45.4 us  [shifted(): lax.ppermute(value, AXES, [(source, source + steps) for source in range(i...]
  transfers between devices with their start and end apart: 14 -> 14, of which waited for: 7 -> 6; matrix products, arithmetic and copies ran while one was open for 0% -> 0% of each run, Pallas kernels for 16% -> 17%
where the time goes in v3:
time: 127 us
  waiting for transfers between devices  54 us (43%)
  starting transfers between devices  45.4 us (36%)
  Pallas kernels  23.8 us (19%)
  local copies, waits for them, and re-layouts  3.44 us (3%)
    ppermute x14, waiting for transfers between devices, shifted(): lax.ppermute(value, AXES, [(source, source + steps) for source in range(i...  54 us
    ppermute x14, starting transfers between devices, shifted(): lax.ppermute(value, AXES, [(source, source + steps) for source in range(i...  45.4 us
    pallas_call x10, Pallas kernels, call(): pl.pallas_call(kernel, out_shape=[jax.ShapeDtypeStruct(shape, jnp.float32...  23.8 us
    unnamed x18, local copies, waits for them, and re-layouts  3.44 us
  transfers between devices with their start and end apart: 14, of which 6 were waited for; matrix products, arithmetic and copies ran while one was open for 0% of the time, Pallas kernels for 17%

profile of v3, /device:TPU:126, one launch (start us, length us, event | category | flops | bytes accessed | tf_op | source)
XLA Modules:
  0.0 126.9 jit_solution(3678273294787546377)
XLA Ops:
  0.0 2.6 %collective-permute-start.3 = (f32[512,128]{1,0:T(8,128)}, f32[512,128]{1,0:T(8,128)S(1)}, u32[]{:S(2)}, u32[]{:S(2)}) collective-permute-start(f32[512,128]{1,0:T(8,128)} %bitcast.20), channel_id=1, source_target_pairs={{1,0},{2,1},{3,2},{4,3},{5,4},{6,5},{7,6},{8,7},{9,8},{10,9},{11,1... | collective-permute-start | bytes 786440 | tf_op jit(solution)/shard_map/ppermute | solution.py:21
  2.6 4.1 %collective-permute-start.2 = (f32[512,128]{1,0:T(8,128)}, f32[512,128]{1,0:T(8,128)S(1)}, u32[]{:S(2)}, u32[]{:S(2)}) collective-permute-start(f32[512,128]{1,0:T(8,128)} %bitcast.21), channel_id=1, source_target_pairs={{0,1},{1,2},{2,3},{3,4},{4,5},{5,6},{6,7},{7,8},{8,9},{9,10},{10,1... | collective-permute-start | bytes 786440 | tf_op jit(solution)/shard_map/ppermute | solution.py:21
  6.8 6.8 %shard_map.55 = (f32[512,512]{1,0:T(8,128)}, f32[512,512]{1,0:T(8,128)}, f32[512,128]{1,0:T(8,128)}) custom-call(f32[512,512]{1,0:T(8,128)} %bitcast.16, f32[512,512]{1,0:T(8,128)} %bitcast.6, f32[512,512]{1,0:T(8,128)} %bitcast.11, f32[512,128]{1,0:T(8,128)} %bitcast.18), custom_call_target="tpu_custom_call" | custom-call | tf_op jit(solution)/shard_map/pallas_call | solution.py:144
  13.6 1.9 %collective-permute-start.1 = (f32[512,512]{1,0:T(8,128)}, f32[512,512]{1,0:T(8,128)S(1)}, u32[]{:S(2)}, u32[]{:S(2)}) collective-permute-start(f32[512,512]{1,0:T(8,128)} %get-tuple-element.42.scaled_low.left.left_a), channel_id=1, source_target_pairs={{1,0},{2,1},{3,2},{4,3},{5,4},{6,5},{7,6},{8,7},{9,8},{10,9},{11,1... | collective-permute-start | bytes 3145736 | tf_op jit(solution)/shard_map/ppermute | solution.py:21
  15.5 4.9 %collective-permute-start = (f32[512,512]{1,0:T(8,128)}, f32[512,512]{1,0:T(8,128)S(1)}, u32[]{:S(2)}, u32[]{:S(2)}) collective-permute-start(f32[512,512]{1,0:T(8,128)} %get-tuple-element.44.scaled_up.left.left_b), channel_id=1, source_target_pairs={{0,1},{1,2},{2,3},{3,4},{4,5},{5,6},{6,7},{7,8},{8,9},{9,10},{10,1... | collective-permute-start | bytes 3145736 | tf_op jit(solution)/shard_map/ppermute | solution.py:21
  20.4 0.0 collective-permute-done.3.guess_r
  20.4 0.0 collective-permute-done.2.guess_l
  20.4 0.0 copy-start.3
  20.4 1.2 copy-done.3
  21.7 0.0 copy-start.5
  21.7 1.2 copy-done.5
  22.9 0.0 copy-start.8
  22.9 0.9 copy-done.8
  23.9 0.0 copy-start
  23.9 0.0 copy-start.1
  23.9 0.0 copy-start.2
  23.9 0.7 shard_map.56
  24.6 17.8 %collective-permute-done.1.low_r.third = f32[512,512]{1,0:T(8,128)S(1)} collective-permute-done((f32[512,512]{1,0:T(8,128)}, f32[512,512]{1,0:T(8,128)S(1)}, u32[]{:S(2)}, u32[]{:S(2)}) %collective-permute-start.1) | collective-permute-done | bytes 1048608 | tf_op jit(solution)/shard_map/ppermute | solution.py:21
  42.4 0.0 copy-start.7
  42.4 2.0 %collective-permute-start.4 = (f32[512,256]{1,0:T(8,128)S(1)}, f32[512,256]{1,0:T(8,128)S(1)}, u32[]{:S(2)}, u32[]{:S(2)}) collective-permute-start(f32[512,256]{1,0:T(8,128)S(1)} %get-tuple-element.38), channel_id=1, source_target_pairs={{0,1},{1,2},{2,3},{3,4},{4,5},{5,6},{6,7},{7,8},{8,9},{9,10},{10,1... | collective-permute-start | bytes 1572872 | tf_op jit(solution)/shard_map/ppermute | solution.py:21
  44.4 3.9 %collective-permute-start.5 = (f32[512,256]{1,0:T(8,128)S(1)}, f32[512,256]{1,0:T(8,128)S(1)}, u32[]{:S(2)}, u32[]{:S(2)}) collective-permute-start(f32[512,256]{1,0:T(8,128)S(1)} %get-tuple-element.39), channel_id=1, source_target_pairs={{1,0},{2,1},{3,2},{4,3},{5,4},{6,5},{7,6},{8,7},{9,8},{10,9},{11,1... | collective-permute-start | bytes 1572872 | tf_op jit(solution)/shard_map/ppermute | solution.py:21
  48.4 0.0 collective-permute-done.up_l.third
  48.4 0.0 copy-done
  48.4 0.0 copy-done.1
  48.4 0.0 copy-done.2
  48.4 5.6 %shard_map.57 = (f32[512,512]{1,0:T(8,128)S(1)}, f32[512,512]{1,0:T(8,128)S(1)}, f32[512,512]{1,0:T(8,128)S(1)}, f32[512,512]{1,0:T(8,128)S(1)}) custom-call(f32[512,512]{1,0:T(8,128)S(1)} %bitcast.17, f32[512,512]{1,0:T(8,128)S(1)} %bitcast.7, f32[512,512]{1,0:T(8,128)S(1)} %bitcast.12, f32[512,512]{1,0:T(8,128)S(1)} %collective-permute-done.up_l.third, ...), custom_call_target="tpu_custom_call" | custom-call | tf_op jit(solution)/shard_map/pallas_call | solution.py:144
  54.0 2.9 %collective-permute-start.8 = (f32[512,512]{1,0:T(8,128)S(1)}, f32[512,512]{1,0:T(8,128)S(1)}, u32[]{:S(2)}, u32[]{:S(2)}) collective-permute-start(f32[512,512]{1,0:T(8,128)S(1)} %get-tuple-element.43), channel_id=1, source_target_pairs={{0,1},{1,2},{2,3},{3,4},{4,5},{5,6},{6,7},{7,8},{8,9},{9,10},{10,1... | collective-permute-start | bytes 3145736 | tf_op jit(solution)/shard_map/ppermute | solution.py:21
  56.9 3.0 %collective-permute-start.9 = (f32[512,512]{1,0:T(8,128)S(1)}, f32[512,512]{1,0:T(8,128)S(1)}, u32[]{:S(2)}, u32[]{:S(2)}) collective-permute-start(f32[512,512]{1,0:T(8,128)S(1)} %get-tuple-element.45), channel_id=1, source_target_pairs={{1,0},{2,1},{3,2},{4,3},{5,4},{6,5},{7,6},{8,7},{9,8},{10,9},{11,1... | collective-permute-start | bytes 3145736 | tf_op jit(solution)/shard_map/ppermute | solution.py:21
  59.9 0.0 collective-permute-done.4.vec_l
  59.9 0.0 collective-permute-done.5.vec_r
  59.9 0.0 copy-done.7
  59.9 0.0 copy-start.6
  59.9 1.6 %shard_map.58 = (f32[512,128]{1,0:T(8,128)S(1)}, f32[512,128]{1,0:T(8,128)S(1)}, f32[512,128]{1,0:T(8,128)S(1)}) custom-call(f32[512,512]{1,0:T(8,128)S(1)} %bitcast.8, f32[512,512]{1,0:T(8,128)S(1)} %bitcast.13, f32[512,128]{1,0:T(8,128)S(1)} %bitcast.19, f32[512,512]{1,0:T(8,128)S(1)} %get-tuple-element.37.pivot1, ...), custom_call_target="tpu_custom_call" | custom-call | flops 10000000000 | tf_op jit(solution)/shard_map/pallas_call | solution.py:144
  61.6 3.8 %collective-permute-start.6 = (f32[512,128]{1,0:T(8,128)S(1)}, f32[512,128]{1,0:T(8,128)S(1)}, u32[]{:S(2)}, u32[]{:S(2)}) collective-permute-start(f32[512,128]{1,0:T(8,128)S(1)} %get-tuple-element.40), channel_id=1, source_target_pairs={{0,1},{1,2},{2,3},{3,4},{4,5},{5,6},{6,7},{7,8},{8,9},{9,10},{10,1... | collective-permute-start | bytes 786440 | tf_op jit(solution)/shard_map/ppermute | solution.py:21
  65.4 0.0 copy-start.4
  65.4 2.2 %collective-permute-start.7 = (f32[512,128]{1,0:T(8,128)S(1)}, f32[512,128]{1,0:T(8,128)S(1)}, u32[]{:S(2)}, u32[]{:S(2)}) collective-permute-start(f32[512,128]{1,0:T(8,128)S(1)} %get-tuple-element.41), channel_id=1, source_target_pairs={{1,0},{2,1},{3,2},{4,3},{5,4},{6,5},{7,6},{8,7},{9,8},{10,9},{11,1... | collective-permute-start | bytes 786440 | tf_op jit(solution)/shard_map/ppermute | solution.py:21
  67.6 15.7 %collective-permute-done.8.right = f32[512,512]{1,0:T(8,128)S(1)} collective-permute-done((f32[512,512]{1,0:T(8,128)S(1)}, f32[512,512]{1,0:T(8,128)S(1)}, u32[]{:S(2)}, u32[]{:S(2)}) %collective-permute-start.8) | collective-permute-done | bytes 1048608 | tf_op jit(solution)/shard_map/ppermute | solution.py:21
  83.2 0.0 copy-done.6
  83.2 1.0 shard_map.59
  84.2 5.0 %collective-permute-start.12 = (f32[512,512]{1,0:T(8,128)S(1)}, f32[512,512]{1,0:T(8,128)S(1)}, u32[]{:S(2)}, u32[]{:S(2)}) collective-permute-start(f32[512,512]{1,0:T(8,128)S(1)} %shard_map.59), channel_id=1, source_target_pairs={{0,1},{1,2},{2,3},{3,4},{4,5},{5,6},{6,7},{7,8},{8,9},{9,10},{10,1... | collective-permute-start | bytes 3145736 | tf_op jit(solution)/shard_map/ppermute | solution.py:21
  89.3 0.0 collective-permute-done.9.right
  89.3 0.0 copy-done.4
  89.3 1.0 shard_map.60
  90.3 2.1 %collective-permute-start.13 = (f32[512,512]{1,0:T(8,128)S(1)}, f32[512,512]{1,0:T(8,128)S(1)}, u32[]{:S(2)}, u32[]{:S(2)}) collective-permute-start(f32[512,512]{1,0:T(8,128)S(1)} %shard_map.60), channel_id=1, source_target_pairs={{1,0},{2,1},{3,2},{4,3},{5,4},{6,5},{7,6},{8,7},{9,8},{10,9},{11,1... | collective-permute-start | bytes 3145736 | tf_op jit(solution)/shard_map/ppermute | solution.py:21
  92.4 7.7 %collective-permute-done.6.right_a = f32[512,128]{1,0:T(8,128)S(1)} collective-permute-done((f32[512,128]{1,0:T(8,128)S(1)}, f32[512,128]{1,0:T(8,128)S(1)}, u32[]{:S(2)}, u32[]{:S(2)}) %collective-permute-start.6) | collective-permute-done | bytes 262176 | tf_op jit(solution)/shard_map/ppermute | solution.py:21
  100.1 0.0 collective-permute-done.7.right_b
  100.1 0.7 shard_map.61
  100.8 5.0 %collective-permute-start.10 = (f32[512,128]{1,0:T(8,128)S(1)}, f32[512,128]{1,0:T(8,128)S(1)}, u32[]{:S(2)}, u32[]{:S(2)}) collective-permute-start(f32[512,128]{1,0:T(8,128)S(1)} %get-tuple-element.48), channel_id=1, source_target_pairs={{0,1},{1,2},{2,3},{3,4},{4,5},{5,6},{6,7},{7,8},{8,9},{9,10},{10,1... | collective-permute-start | bytes 786440 | tf_op jit(solution)/shard_map/ppermute | solution.py:21
  105.8 1.9 %collective-permute-start.11 = (f32[512,128]{1,0:T(8,128)S(1)}, f32[512,128]{1,0:T(8,128)S(1)}, u32[]{:S(2)}, u32[]{:S(2)}) collective-permute-start(f32[512,128]{1,0:T(8,128)S(1)} %get-tuple-element.49), channel_id=1, source_target_pairs={{1,0},{2,1},{3,2},{4,3},{5,4},{6,5},{7,6},{8,7},{9,8},{10,9},{11,1... | collective-permute-start | bytes 786440 | tf_op jit(solution)/shard_map/ppermute | solution.py:21
  107.8 3.5 %collective-permute-done.12.second = f32[512,512]{1,0:T(8,128)S(1)} collective-permute-done((f32[512,512]{1,0:T(8,128)S(1)}, f32[512,512]{1,0:T(8,128)S(1)}, u32[]{:S(2)}, u32[]{:S(2)}) %collective-permute-start.12) | collective-permute-done | bytes 1048608 | tf_op jit(solution)/shard_map/ppermute | solution.py:21
  111.3 1.8 %shard_map.62.base = f32[512,512]{1,0:T(8,128)S(1)} custom-call(f32[512,512]{1,0:T(8,128)S(1)} %get-tuple-element.50.base, f32[512,512]{1,0:T(8,128)S(1)} %bitcast.9, f32[512,512]{1,0:T(8,128)S(1)} %collective-permute-done.12.second, f32[512,512]{1,0:T(8,128)S(1)} %collective-permute-done.up_l.third), custom_call_target="tpu_custom_call" | custom-call | tf_op jit(solution)/shard_map/pallas_call | solution.py:144
  113.1 8.5 %collective-permute-done.13.second = f32[512,512]{1,0:T(8,128)S(1)} collective-permute-done((f32[512,512]{1,0:T(8,128)S(1)}, f32[512,512]{1,0:T(8,128)S(1)}, u32[]{:S(2)}, u32[]{:S(2)}) %collective-permute-start.13) | collective-permute-done | bytes 1048608 | tf_op jit(solution)/shard_map/ppermute | solution.py:21
  121.6 2.1 %shard_map.63 = (f32[512,512]{1,0:T(8,128)S(1)}, f32[8,128]{1,0:T(8,128)S(1)}) custom-call(f32[512,512]{1,0:T(8,128)S(1)} %shard_map.62.base, f32[512,512]{1,0:T(8,128)S(1)} %bitcast.14, f32[512,512]{1,0:T(8,128)S(1)} %collective-permute-done.13.second, f32[512,512]{1,0:T(8,128)S(1)} %collective-permute-done.1.low_r.third), custom_call_target="tpu_custom_call" | custom-call | tf_op jit(solution)/shard_map/pallas_call | solution.py:144
  123.7 0.0 collective-permute-done.10.d_l
  123.8 0.7 collective-permute-done.11.d_r
  124.5 2.5 %shard_map.64 = f32[512,128]{1,0:T(8,128)} custom-call(f32[512,512]{1,0:T(8,128)S(1)} %get-tuple-element.52.rest, f32[8,128]{1,0:T(8,128)S(1)} %get-tuple-element.53.scale, f32[512,128]{1,0:T(8,128)S(1)} %get-tuple-element.54.rhs1, f32[512,512]{1,0:T(8,128)S(1)} %bitcast.10, f32[512,512]{1,0:T(8,128)S(1)} %bitcast.15, ...), custom_call_target="tpu_custom_call" | custom-call | tf_op jit(solution)/shard_map/pallas_call | solution.py:144
Async XLA Ops:
  0.0 20.4 %collective-permute-start.3 = (f32[512,128]{1,0:T(8,128)}, f32[512,128]{1,0:T(8,128)S(1)}, u32[]{:S(2)}, u32[]{:S(2)}) collective-permute-start(f32[512,128]{1,0:T(8,128)} %bitcast.20), channel_id=1, source_target_pairs={{1,0},{2,1},{3,2},{4,3},{5,4},{6,5},{7,6},{8,7},{9,8},{10,9},{11,1... | collective-permute-start | bytes 786440 | tf_op jit(solution)/shard_map/ppermute | solution.py:21
  2.6 17.8 %collective-permute-start.2 = (f32[512,128]{1,0:T(8,128)}, f32[512,128]{1,0:T(8,128)S(1)}, u32[]{:S(2)}, u32[]{:S(2)}) collective-permute-start(f32[512,128]{1,0:T(8,128)} %bitcast.21), channel_id=1, source_target_pairs={{0,1},{1,2},{2,3},{3,4},{4,5},{5,6},{6,7},{7,8},{8,9},{9,10},{10,1... | collective-permute-start | bytes 786440 | tf_op jit(solution)/shard_map/ppermute | solution.py:21
  13.6 28.8 %collective-permute-start.1 = (f32[512,512]{1,0:T(8,128)}, f32[512,512]{1,0:T(8,128)S(1)}, u32[]{:S(2)}, u32[]{:S(2)}) collective-permute-start(f32[512,512]{1,0:T(8,128)} %get-tuple-element.42.scaled_low.left.left_a), channel_id=1, source_target_pairs={{1,0},{2,1},{3,2},{4,3},{5,4},{6,5},{7,6},{8,7},{9,8},{10,9},{11,1... | collective-permute-start | bytes 3145736 | tf_op jit(solution)/shard_map/ppermute | solution.py:21
  15.5 32.8 %collective-permute-start = (f32[512,512]{1,0:T(8,128)}, f32[512,512]{1,0:T(8,128)S(1)}, u32[]{:S(2)}, u32[]{:S(2)}) collective-permute-start(f32[512,512]{1,0:T(8,128)} %get-tuple-element.44.scaled_up.left.left_b), channel_id=1, source_target_pairs={{0,1},{1,2},{2,3},{3,4},{4,5},{5,6},{6,7},{7,8},{8,9},{9,10},{10,1... | collective-permute-start | bytes 3145736 | tf_op jit(solution)/shard_map/ppermute | solution.py:21
  20.4 1.3 copy-start.3
  21.7 1.2 copy-start.5
  22.9 0.9 copy-start.8
  23.9 24.5 %copy-start = (f32[1,512,512]{2,1,0:T(8,128)S(1)}, f32[1,512,512]{2,1,0:T(8,128)}, u32[]{:S(2)}) copy-start(f32[1,512,512]{2,1,0:T(8,128)} %param.6) | copy-start | bytes 3145732
  23.9 24.5 %copy-start.1 = (f32[1,512,512]{2,1,0:T(8,128)S(1)}, f32[1,512,512]{2,1,0:T(8,128)}, u32[]{:S(2)}) copy-start(f32[1,512,512]{2,1,0:T(8,128)} %param.7) | copy-start | bytes 3145732
  23.9 24.5 %copy-start.2 = (f32[1,512,512]{2,1,0:T(8,128)S(1)}, f32[1,512,512]{2,1,0:T(8,128)}, u32[]{:S(2)}) copy-start(f32[1,512,512]{2,1,0:T(8,128)} %param.5) | copy-start | bytes 3145732
  42.4 17.5 %copy-start.7 = (f32[1,512,128]{2,1,0:T(8,128)S(1)}, f32[1,512,128]{2,1,0:T(8,128)}, u32[]{:S(2)}) copy-start(f32[1,512,128]{2,1,0:T(8,128)} %param.8) | copy-start | bytes 786436
  42.4 17.5 %collective-permute-start.4 = (f32[512,256]{1,0:T(8,128)S(1)}, f32[512,256]{1,0:T(8,128)S(1)}, u32[]{:S(2)}, u32[]{:S(2)}) collective-permute-start(f32[512,256]{1,0:T(8,128)S(1)} %get-tuple-element.38), channel_id=1, source_target_pairs={{0,1},{1,2},{2,3},{3,4},{4,5},{5,6},{6,7},{7,8},{8,9},{9,10},{10,1... | collective-permute-start | bytes 1572872 | tf_op jit(solution)/shard_map/ppermute | solution.py:21
  44.4 15.5 %collective-permute-start.5 = (f32[512,256]{1,0:T(8,128)S(1)}, f32[512,256]{1,0:T(8,128)S(1)}, u32[]{:S(2)}, u32[]{:S(2)}) collective-permute-start(f32[512,256]{1,0:T(8,128)S(1)} %get-tuple-element.39), channel_id=1, source_target_pairs={{1,0},{2,1},{3,2},{4,3},{5,4},{6,5},{7,6},{8,7},{9,8},{10,9},{11,1... | collective-permute-start | bytes 1572872 | tf_op jit(solution)/shard_map/ppermute | solution.py:21
  54.0 29.2 %collective-permute-start.8 = (f32[512,512]{1,0:T(8,128)S(1)}, f32[512,512]{1,0:T(8,128)S(1)}, u32[]{:S(2)}, u32[]{:S(2)}) collective-permute-start(f32[512,512]{1,0:T(8,128)S(1)} %get-tuple-element.43), channel_id=1, source_target_pairs={{0,1},{1,2},{2,3},{3,4},{4,5},{5,6},{6,7},{7,8},{8,9},{9,10},{10,1... | collective-permute-start | bytes 3145736 | tf_op jit(solution)/shard_map/ppermute | solution.py:21
  56.9 32.4 %collective-permute-start.9 = (f32[512,512]{1,0:T(8,128)S(1)}, f32[512,512]{1,0:T(8,128)S(1)}, u32[]{:S(2)}, u32[]{:S(2)}) collective-permute-start(f32[512,512]{1,0:T(8,128)S(1)} %get-tuple-element.45), channel_id=1, source_target_pairs={{1,0},{2,1},{3,2},{4,3},{5,4},{6,5},{7,6},{8,7},{9,8},{10,9},{11,1... | collective-permute-start | bytes 3145736 | tf_op jit(solution)/shard_map/ppermute | solution.py:21
  59.9 23.3 %copy-start.6 = (f32[512,512]{1,0:T(8,128)S(1)}, f32[512,512]{1,0:T(8,128)}, u32[]{:S(2)}) copy-start(f32[512,512]{1,0:T(8,128)} %get-tuple-element.42.scaled_low.left.left_a) | copy-start | bytes 3145732
  61.6 38.5 %collective-permute-start.6 = (f32[512,128]{1,0:T(8,128)S(1)}, f32[512,128]{1,0:T(8,128)S(1)}, u32[]{:S(2)}, u32[]{:S(2)}) collective-permute-start(f32[512,128]{1,0:T(8,128)S(1)} %get-tuple-element.40), channel_id=1, source_target_pairs={{0,1},{1,2},{2,3},{3,4},{4,5},{5,6},{6,7},{7,8},{8,9},{9,10},{10,1... | collective-permute-start | bytes 786440 | tf_op jit(solution)/shard_map/ppermute | solution.py:21
  65.4 23.9 %copy-start.4 = (f32[512,512]{1,0:T(8,128)S(1)}, f32[512,512]{1,0:T(8,128)}, u32[]{:S(2)}) copy-start(f32[512,512]{1,0:T(8,128)} %get-tuple-element.44.scaled_up.left.left_b) | copy-start | bytes 3145732
  65.4 34.7 %collective-permute-start.7 = (f32[512,128]{1,0:T(8,128)S(1)}, f32[512,128]{1,0:T(8,128)S(1)}, u32[]{:S(2)}, u32[]{:S(2)}) collective-permute-start(f32[512,128]{1,0:T(8,128)S(1)} %get-tuple-element.41), channel_id=1, source_target_pairs={{1,0},{2,1},{3,2},{4,3},{5,4},{6,5},{7,6},{8,7},{9,8},{10,9},{11,1... | collective-permute-start | bytes 786440 | tf_op jit(solution)/shard_map/ppermute | solution.py:21
  84.2 27.1 %collective-permute-start.12 = (f32[512,512]{1,0:T(8,128)S(1)}, f32[512,512]{1,0:T(8,128)S(1)}, u32[]{:S(2)}, u32[]{:S(2)}) collective-permute-start(f32[512,512]{1,0:T(8,128)S(1)} %shard_map.59), channel_id=1, source_target_pairs={{0,1},{1,2},{2,3},{3,4},{4,5},{5,6},{6,7},{7,8},{8,9},{9,10},{10,1... | collective-permute-start | bytes 3145736 | tf_op jit(solution)/shard_map/ppermute | solution.py:21
  90.3 31.4 %collective-permute-start.13 = (f32[512,512]{1,0:T(8,128)S(1)}, f32[512,512]{1,0:T(8,128)S(1)}, u32[]{:S(2)}, u32[]{:S(2)}) collective-permute-start(f32[512,512]{1,0:T(8,128)S(1)} %shard_map.60), channel_id=1, source_target_pairs={{1,0},{2,1},{3,2},{4,3},{5,4},{6,5},{7,6},{8,7},{9,8},{10,9},{11,1... | collective-permute-start | bytes 3145736 | tf_op jit(solution)/shard_map/ppermute | solution.py:21
  100.8 22.9 %collective-permute-start.10 = (f32[512,128]{1,0:T(8,128)S(1)}, f32[512,128]{1,0:T(8,128)S(1)}, u32[]{:S(2)}, u32[]{:S(2)}) collective-permute-start(f32[512,128]{1,0:T(8,128)S(1)} %get-tuple-element.48), channel_id=1, source_target_pairs={{0,1},{1,2},{2,3},{3,4},{4,5},{5,6},{6,7},{7,8},{8,9},{9,10},{10,1... | collective-permute-start | bytes 786440 | tf_op jit(solution)/shard_map/ppermute | solution.py:21
  105.8 18.6 %collective-permute-start.11 = (f32[512,128]{1,0:T(8,128)S(1)}, f32[512,128]{1,0:T(8,128)S(1)}, u32[]{:S(2)}, u32[]{:S(2)}) collective-permute-start(f32[512,128]{1,0:T(8,128)S(1)} %get-tuple-element.49), channel_id=1, source_target_pairs={{1,0},{2,1},{3,2},{4,3},{5,4},{6,5},{7,6},{8,7},{9,8},{10,9},{11,1... | collective-permute-start | bytes 786440 | tf_op jit(solution)/shard_map/ppermute | solution.py:21
